TPU v7x, 32 devices: a whole 2x2x4 slice. The times are simulated.
32 devices in a mesh: shard: 8 (over z, y), grp: 4 (over x, core).
Axes of the slice: x: 2, y: 2, z: 4, core: 2. Of those that a mesh axis runs over, the one named last changes fastest.
Arguments:
- entity_table: float32 [131072, 400], P(('shard', 'grp')), may hold values from -1.5 to 1.5
- rel_diag: float32 [64, 400], replicated, may hold values from 0.25 to 1.75
- src_ids: int32 [64000], P(('shard', 'grp')), may hold values from 0 to 131071, as said below
- dst_ids: int32 [64000], P(('shard', 'grp')), may hold values from 0 to 131071, as said below
- rel_ids: int32 [64000], P(('shard', 'grp')), may hold values from 0 to 63
- neg_ids: int32 [16, 1000], P('shard'), may hold values from 0 to 131071, as said below
Outputs:
- entity_grad: float32 [131072, 400], P(('shard', 'grp'))
Inputs may be any that keep to these rules, and one draw needn't show every extreme that they name: `src_ids`: entity e is held by device e // 4096 of shard+grp. Among the sources and destinations of the 2000 edges of one device (aligned blocks of 2000 edges), at most 250 are held by any one device; in every draw one device holds exactly 250 of those of every block. `dst_ids`: drawn together with src_ids, under the bound stated there. `neg_ids`: for a shard index s and a column block g (columns g * 250 to (g + 1) * 250 - 1), the entries of rows s * 2 to (s + 1) * 2 - 1 in that block name at most 31 entities held by any one device; in every draw one device holds exactly 31 of those of every such block. A whole row set s thus names at most 124 of one device's entities, reached.
All inputs are finite; a program needn't handle non-finite values.
Results may differ from a plain program's by a relative error of at most 0.0037.
Values may be sent and summed in bfloat16 or wider, within the bound.
No kernel may reach another device: no remote copies, remote signals or barrier semaphores. Data moves between devices by JAX's collectives and lax.ppermute only.
A program may use at most 192 MiB of HBM per device.

v0:
```python
import functools

import jax
import jax.numpy as jnp
from jax import lax
from jax.experimental import pallas as pl
from jax.experimental.pallas import tpu as pltpu
from jax.sharding import PartitionSpec as P

LANES = 128
POOL = 48
RELAYS = 4
SMALL = 80
PARTS = 4
SHARE = LANES // PARTS
VMEM_BYTES = 56 << 20
F32 = jnp.float32
BF16 = jnp.bfloat16
NN = (((1,), (0,)), ((), ()))
NT = (((1,), (1,)), ((), ()))
TN = (((0,), (0,)), ((), ()))


def round_up(value, unit):
    return -(-value // unit) * unit


def dot(left, right, dims):
    return lax.dot_general(left, right, dims, preferred_element_type=F32)


def one_hot(rows, row, base=0):
    places = lax.broadcasted_iota(jnp.int32, (rows, row.shape[1]), 0) + base
    return jnp.where(places == row, 1.0, 0.0).astype(BF16)


def call(kernel, name, flops, nbytes, **kwargs):
    return pl.pallas_call(
        kernel,
        name=name,
        compiler_params=pltpu.CompilerParams(vmem_limit_bytes=VMEM_BYTES),
        cost_estimate=pl.CostEstimate(flops=flops, bytes_accessed=nbytes, transcendentals=0),
        **kwargs,
    )


def ranks(members, mixer):
    groups = members[0].shape[0]
    both = dot(jnp.concatenate(members, axis=0).astype(BF16), mixer, NN)
    taken = jnp.zeros((groups, LANES), F32)
    found = []
    for i, member in enumerate(members):
        chunk = both[i * groups : (i + 1) * groups]
        found.append(jnp.sum((chunk[:, :LANES] + taken) * member, axis=0, keepdims=True))
        taken = taken + chunk[:, LANES:]
    return [rank.astype(jnp.int32) for rank in found], taken


def fill(members, codes, places, count):
    groups = members[0].shape[0]
    high = [m * (c // LANES).astype(F32) for m, c in zip(members, codes)]
    low = [m * (c % LANES).astype(F32) for m, c in zip(members, codes)]
    left = jnp.concatenate(
        [jnp.concatenate(high, axis=1), jnp.concatenate(low, axis=1)], axis=0
    ).astype(BF16)
    sums = dot(left, one_hot(count, jnp.concatenate(places, axis=1)), NT)
    return (LANES * sums[:groups] + sums[groups:]).astype(jnp.int32) - 1


def slots_kernel(
    me_ref, src_ref, dst_ref, own_ref, *refs, rows_dev, devices, chunks, neg_cap, spans, part
):
    pooled = chunks == 0
    msg_ref, neg_ref = refs[0], refs[-1]
    slot_refs = refs[1:-1]
    row = lax.broadcasted_iota(jnp.int32, (LANES, 2 * LANES), 0)
    lane = lax.broadcasted_iota(jnp.int32, (LANES, 2 * LANES), 1)
    mixer = jnp.where(row < lane, 1.0, 0.0).astype(BF16)
    owners = lax.broadcasted_iota(jnp.int32, (devices, LANES), 0)

    def prepare(rows, width):
        where, holder, codes, members = [], [], [], []
        for segment, ids_row in enumerate(rows):
            blank = jnp.full((1, width - ids_row.shape[1]), -1, jnp.int32)
            ids_row = jnp.concatenate([ids_row, blank], axis=1)
            for start in range(0, width, LANES):
                ids = ids_row[:, start : start + LANES]
                owner = jnp.where(ids >= 0, ids // rows_dev, -1)
                where.append((slice(segment, segment + 1), slice(start, start + LANES)))
                holder.append(owner)
                codes.append(jnp.where(ids >= 0, ids - owner * rows_dev + 1, 0))
                members.append(jnp.where(owners == owner, 1.0, 0.0))
        return where, holder, codes, members

    ends = []
    for ids_ref in (src_ref, dst_ref):
        ids = ids_ref[...].reshape(1, ids_ref.shape[0])
        length = ids.shape[1] // spans
        ends += [ids[:, b * length : (b + 1) * length] for b in range(spans)]
    where, holder, codes, members = prepare(ends, slot_refs[0].shape[1])
    flag = jnp.full((1, 1), -1, jnp.int32)
    if pooled:
        turn = me_ref[0, 0] % PARTS
        quarters = [jnp.maximum(code - 1, 0) // (rows_dev // PARTS) for code in codes]
        split = [
            jnp.concatenate([jnp.where(q == k, member, 0.0) for k in range(PARTS)], axis=0)
            for member, q in zip(members, quarters)
        ]
        found, _ = ranks(split, mixer)
        places = []
        for at, owner, rank, q in zip(where, holder, found, quarters):
            inside = (owner >= 0) & (rank < SHARE)
            place = (q ^ turn) * SHARE + rank
            slot_refs[0][at] = jnp.where(inside, owner * LANES + place, -1)
            places.append(jnp.where(inside, place, -1))
        msg_ref[:, :LANES] = fill(members, codes, places, LANES)
        offset = LANES

        pool_ref, busy_ref = slot_refs[1:]
        shards = devices // RELAYS
        room = RELAYS * POOL
        shard_rows = lax.broadcasted_iota(jnp.int32, (shards, LANES), 0)
        spilled, spill_codes = [], []
        for owner, code, rank in zip(holder, codes, found):
            shard = jnp.where(rank >= SHARE, owner // RELAYS, -1)
            spilled.append(jnp.where(shard_rows == shard, 1.0, 0.0))
            spill_codes.append(code + (owner % RELAYS) * rows_dev)
        listed, taken = ranks(spilled, mixer)
        places = []
        for at, owner, rank, place in zip(where, holder, found, listed):
            inside = (owner >= 0) & (rank >= SHARE) & (place < room)
            compact = jnp.where(
                place < SMALL, owner // RELAYS * SMALL + place, (shards - 1) * SMALL + place
            )
            pool_ref[at] = jnp.where(inside, compact, -1)
            places.append(jnp.where(inside, place, -1))
        listed = fill(spilled, spill_codes, places, 2 * LANES)
        for shard in range(shards):
            msg_ref[shard * RELAYS : (shard + 1) * RELAYS, offset : offset + 2 * LANES] = (
                jnp.broadcast_to(listed[shard : shard + 1], (RELAYS, 2 * LANES))
            )
        offset += 2 * LANES
        most = jnp.max(taken, axis=0, keepdims=True)
        busy = jnp.where(taken > SMALL, 1.0, 0.0)
        crowded = jnp.sum(busy, axis=0, keepdims=True) > 1.0
        flag = jnp.where((most > room) | crowded, 1, -1)[:, :1]
        place = jnp.sum(busy * shard_rows.astype(F32), axis=0, keepdims=True).astype(jnp.int32)
        busy_ref[...] = jnp.minimum(place, shards - 1)[:, :1]
    else:
        found, _ = ranks(members, mixer)
        for chunk in range(chunks):
            places = []
            for at, owner, rank in zip(where, holder, found):
                place = rank - chunk * LANES
                place = jnp.where((owner >= 0) & (place >= 0) & (place < LANES), place, -1)
                slot_refs[chunk][at] = jnp.where(place >= 0, owner * LANES + place, -1)
                places.append(place)
            msg_ref[:, chunk * LANES : (chunk + 1) * LANES] = fill(members, codes, places, LANES)
        offset = chunks * LANES

    where, holder, codes, members = prepare([own_ref[b : b + 1, :] for b in range(spans)], part)
    found, _ = ranks(members, mixer)
    for at, owner, rank in zip(where, holder, found):
        neg_ref[at] = jnp.where(owner >= 0, owner * neg_cap + rank, -1)
    places = [jnp.where(owner >= 0, rank, -1) for owner, rank in zip(holder, found)]
    listed = fill(members, codes, places, LANES)
    lanes = lax.broadcasted_iota(jnp.int32, listed.shape, 1)
    msg_ref[:, offset:] = jnp.where(lanes == LANES - 1, flag, listed)


def make_slots(me, src_ids, dst_ids, own, rows_dev, devices, chunks, neg_cap, width, part):
    lanes = (chunks + 1 if chunks else 4) * LANES
    spans = own.shape[0]
    ends_shape = jax.ShapeDtypeStruct((2 * spans, width), jnp.int32)
    if chunks:
        slots = [ends_shape] * chunks
    else:
        slots = [ends_shape, ends_shape, jax.ShapeDtypeStruct((1, 1), jnp.int32)]
    return call(
        functools.partial(
            slots_kernel,
            rows_dev=rows_dev,
            devices=devices,
            chunks=chunks,
            neg_cap=neg_cap,
            spans=spans,
            part=part,
        ),
        "slots",
        32 * devices * LANES * spans * width,
        16 * spans * width,
        in_specs=[
            pl.BlockSpec(memory_space=pltpu.SMEM),
            pl.BlockSpec(src_ids.shape, lambda: (0,)),
            pl.BlockSpec(dst_ids.shape, lambda: (0,)),
            pl.BlockSpec(own.shape, lambda: (0, 0)),
        ],
        out_shape=[jax.ShapeDtypeStruct((devices, lanes), jnp.int32)]
        + slots
        + [jax.ShapeDtypeStruct((spans, part), jnp.int32)],
    )(me.reshape(1, 1), src_ids, dst_ids, own)


def packed_height(count, feature):
    return feature // LANES * count + feature % LANES


def pack(out_ref, at, start, rows, tail):
    count, feature = rows.shape
    for piece in range(feature // LANES):
        out_ref[at, start + piece * count : start + (piece + 1) * count, :] = rows[
            :, piece * LANES : (piece + 1) * LANES
        ].astype(out_ref.dtype)
    tail = jnp.concatenate([tail, jnp.zeros((tail.shape[0], LANES - count), tail.dtype)], axis=1)
    end = start + packed_height(count, feature)
    out_ref[at, end - tail.shape[0] : end, :] = tail.astype(out_ref.dtype)


def pack_all(out_ref, start, count, rows, turned):
    feature = rows.shape[1]
    first = feature // LANES * LANES
    for i in range(out_ref.shape[0]):
        at = slice(i * count, (i + 1) * count)
        pack(out_ref, i, start, rows[at], turned[first:, at])


def unpack_all(in_ref, start, count, rows_ref, flat_ref):
    feature = flat_ref.shape[0]
    pieces = feature // LANES
    end = start + packed_height(count, feature)
    devices = in_ref.shape[0]
    for d in range(devices):
        for piece in range(pieces):
            rows_ref[d * count : (d + 1) * count, piece * LANES : (piece + 1) * LANES] = in_ref[
                d, start + piece * count : start + (piece + 1) * count, :
            ]
    tails = [
        in_ref[d, end - feature % LANES : end, :].astype(F32)[:, :count] for d in range(devices)
    ]
    flat_ref[: pieces * LANES] = rows_ref[...].astype(F32).T.astype(BF16)
    flat_ref[pieces * LANES :] = jnp.concatenate(tails, axis=1).astype(BF16)


def unpack_scratch(devices, count, feature):
    return [
        pltpu.VMEM((devices * count, feature // LANES * LANES), BF16),
        pltpu.VMEM((feature, devices * count), BF16),
    ]


def gather_kernel(table_ref, *refs, group, neg_cap):
    feature, rows_dev = table_ref.shape
    first = pl.program_id(0) * group
    req_ref, out_ref = refs[0], refs[-1]
    row = [req_ref[pl.ds(first + i, 1), :] for i in range(group)]
    if neg_cap:
        row += [refs[1][pl.ds(first + i, 1), :neg_cap] for i in range(group)]
    rows = dot(table_ref[...], one_hot(rows_dev, jnp.concatenate(row, axis=1)), NN)
    start = out_ref.shape[1] - feature
    for i in range(group):
        out_ref[i, start:] = rows[:, i * LANES : (i + 1) * LANES].astype(BF16)
    if neg_cap:
        neg = rows[:, group * LANES :]
        pack_all(out_ref, 0, neg_cap, neg.T, neg)


def gather(table, requests, neg_requests=None, neg_cap=0):
    feature, rows_dev = table.shape
    devices = requests.shape[0]
    group = 4
    height = feature + (packed_height(neg_cap, feature) if neg_cap else 0)
    slots = devices * (LANES + neg_cap)
    whole = pl.BlockSpec((devices, LANES), lambda i: (0, 0))
    return call(
        functools.partial(gather_kernel, group=group, neg_cap=neg_cap),
        "gather_rows",
        2 * feature * rows_dev * slots,
        2 * feature * (rows_dev + slots),
        grid=(devices // group,),
        in_specs=[pl.BlockSpec((feature, rows_dev), lambda i: (0, 0)), whole]
        + ([whole] if neg_cap else []),
        out_specs=pl.BlockSpec((group, height, LANES), lambda i: (i, 0, 0)),
        out_shape=jax.ShapeDtypeStruct((devices, height, LANES), BF16),
    )(table, requests, *([neg_requests] if neg_cap else []))


def quarter_ids(ids):
    group = lax.broadcasted_iota(jnp.int32, (1, LANES), 1) // SHARE
    rows = []
    for part in range(PARTS):
        pieces = []
        for first in range(0, len(ids), PARTS):
            piece = ids[first + part]
            for j in range(1, PARTS):
                piece = jnp.where(group == j, ids[first + (part ^ j)], piece)
            pieces.append(piece)
        rows.append(jnp.concatenate(pieces, axis=1))
    return rows


def gather_quarters_kernel(table_ref, req_ref, neg_req_ref, out_ref, *, neg_cap):
    feature, rows_dev = table_ref.shape
    group = out_ref.shape[0]
    share = rows_dev // PARTS
    first = pl.program_id(0) * group
    ids = [req_ref[pl.ds(first + i, 1), :] for i in range(group)]
    found = []
    for part, row in enumerate(quarter_ids(ids)):
        start = part * share
        found.append(dot(table_ref[:, start : start + share], one_hot(share, row, start), NN))
    start = out_ref.shape[1] - feature
    lanes = lax.broadcasted_iota(jnp.int32, (feature, LANES), 1) // SHARE
    for i in range(group):
        at = slice(i // PARTS * LANES, (i // PARTS + 1) * LANES)
        rows = found[i % PARTS][:, at]
        for j in range(1, PARTS):
            rows = jnp.where(lanes == j, found[j ^ (i % PARTS)][:, at], rows)
        out_ref[i, start:] = rows.astype(BF16)
    row = [neg_req_ref[pl.ds(first + i, 1), :neg_cap] for i in range(group)]
    neg = dot(table_ref[...], one_hot(rows_dev, jnp.concatenate(row, axis=1)), NN)
    pack_all(out_ref, 0, neg_cap, neg.T, neg)


def gather_quarters(table, requests, neg_requests, neg_cap):
    feature, rows_dev = table.shape
    devices = requests.shape[0]
    group = 16
    height = feature + packed_height(neg_cap, feature)
    whole = pl.BlockSpec((devices, LANES), lambda i: (0, 0))
    return call(
        functools.partial(gather_quarters_kernel, neg_cap=neg_cap),
        "gather_quarters",
        feature * rows_dev * devices * (LANES // 2 + 2 * neg_cap),
        2 * feature * (rows_dev + devices * (LANES + neg_cap)),
        grid=(devices // group,),
        in_specs=[pl.BlockSpec((feature, rows_dev), lambda i: (0, 0)), whole, whole],
        out_specs=pl.BlockSpec((group, height, LANES), lambda i: (i, 0, 0)),
        out_shape=jax.ShapeDtypeStruct((devices, height, LANES), BF16),
    )(table, requests, neg_requests)


def gather_pool_kernel(table_ref, req_ref, out_ref, *, group):
    rows_dev = table_ref.shape[1]
    row = req_ref[...].reshape(1, group * POOL)
    rows = dot(table_ref[...], one_hot(rows_dev, row), NN)
    pack_all(out_ref, 0, POOL, rows.T, rows)


def gather_pool(table, requests, devices):
    feature, rows_dev = table.shape
    group = 8
    steps = devices // group
    height = packed_height(POOL, feature)
    return call(
        functools.partial(gather_pool_kernel, group=group),
        "gather_pool",
        2 * feature * rows_dev * requests.size,
        2 * feature * (rows_dev + requests.size),
        grid=(steps,),
        in_specs=[
            pl.BlockSpec((feature, rows_dev), lambda i: (0, 0)),
            pl.BlockSpec((1, 1, group * POOL), lambda i: (i, 0, 0)),
        ],
        out_specs=pl.BlockSpec((group, height, LANES), lambda i: (i, 0, 0)),
        out_shape=jax.ShapeDtypeStruct((devices, height, LANES), BF16),
    )(table, requests.reshape(steps, 1, group * POOL))


def spread_neg_kernel(back_ref, slot_ref, out_ref, rows, flat, *, cap):
    unpack_all(back_ref, 0, cap, rows, flat)
    for part in range(slot_ref.shape[0]):
        hot = one_hot(flat.shape[1], slot_ref[part : part + 1, :])
        out_ref[part] = dot(flat[...], hot, NN).T.astype(BF16)


def spread_neg(back, slot, cap, feature):
    devices = back.shape[0]
    parts, width = slot.shape
    height = packed_height(cap, feature)
    return call(
        functools.partial(spread_neg_kernel, cap=cap),
        "spread_negatives",
        2 * devices * cap * feature * slot.size,
        2 * devices * cap * feature,
        grid=(1,),
        in_specs=[
            pl.BlockSpec((devices, height, LANES), lambda i: (0, 0, 0)),
            pl.BlockSpec(slot.shape, lambda i: (0, 0)),
        ],
        out_specs=pl.BlockSpec((parts, width, feature), lambda i: (0, 0, 0)),
        out_shape=jax.ShapeDtypeStruct((parts, width, feature), BF16),
        scratch_shapes=unpack_scratch(devices, cap, feature),
    )(back, slot)


def spread_kernel(*refs, first):
    back_ref, slot_ref = refs[:2]
    so_far_ref = None if first else refs[2]
    out_ref, flat = refs[2 + (not first)], refs[-1]
    devices = back_ref.shape[0]
    feature = flat.shape[0]

    @pl.when(pl.program_id(0) == 0)
    def _():
        start = back_ref.shape[1] - feature
        for d in range(devices):
            flat[:, d * LANES : (d + 1) * LANES] = back_ref[d, start:]

    row = slot_ref[...].reshape(1, slot_ref.shape[-1])
    rows = dot(flat[...], one_hot(flat.shape[1], row), NN)
    if not first:
        rows = rows + so_far_ref[...].astype(F32)
    out_ref[...] = rows.astype(BF16)


def spread(back, slot, so_far, feature):
    devices = back.shape[0]
    segments, width = slot.shape
    slots = devices * LANES
    tile = 512 if slots <= 4096 else 128
    steps = width // tile
    rows_spec = pl.BlockSpec((feature, tile), lambda i: (0, i))
    extra = [] if so_far is None else [so_far]
    return call(
        functools.partial(spread_kernel, first=so_far is None),
        "spread_rows",
        2 * feature * slots * slot.size,
        2 * feature * (slots + slot.size),
        grid=(segments * steps,),
        in_specs=[
            pl.BlockSpec(back.shape, lambda i: (0, 0, 0)),
            pl.BlockSpec((1, 1, tile), lambda i: (i // steps, 0, i % steps)),
        ]
        + [rows_spec] * len(extra),
        out_specs=rows_spec,
        out_shape=jax.ShapeDtypeStruct((feature, slot.size), BF16),
        scratch_shapes=[pltpu.VMEM((feature, slots), BF16)],
    )(back, slot.reshape(segments, 1, width), *extra)


def compact_places(shards):
    places = []
    for start, end, whose in ((0, SMALL, range(shards)), (SMALL, RELAYS * POOL, [None])):
        for shard in whose:
            place = start
            while place < end:
                relay, first = place // POOL, place % POOL
                count = min(POOL - first, end - place)
                to = (shards - 1 if shard is None else shard) * SMALL + place
                places.append((shard, relay, first, count, to))
                place += count
    return places


def compact_size(shards):
    return shards * SMALL + RELAYS * POOL - SMALL


def compact_pool(back_ref, busy, rows_ref, flat_ref):
    feature = flat_ref.shape[0]
    pieces = feature // LANES
    tails = []
    for shard, relay, first, count, to in compact_places(back_ref.shape[0] // RELAYS):
        at = (busy if shard is None else shard) * RELAYS + relay
        for piece in range(pieces):
            start = piece * POOL + first
            rows_ref[to : to + count, piece * LANES : (piece + 1) * LANES] = back_ref[
                at, start : start + count, :
            ]
        tail = back_ref[at, pieces * POOL :, :].astype(F32)
        tails.append(tail[:, first : first + count])
    flat_ref[: pieces * LANES] = rows_ref[...].astype(F32).T.astype(BF16)
    flat_ref[pieces * LANES :] = jnp.concatenate(tails, axis=1).astype(BF16)


def expand_pool(rows, busy, out_ref):
    feature = rows.shape[1]
    pieces = feature // LANES
    turned = rows.T
    out_ref[...] = jnp.zeros(out_ref.shape, out_ref.dtype)
    shards = out_ref.shape[0] // RELAYS
    for shard, relay, first, count, to in compact_places(shards):
        at = (busy if shard is None else shard) * RELAYS + relay
        for piece in range(pieces):
            start = piece * POOL + first
            out_ref[at, start : start + count, :] = rows[
                to : to + count, piece * LANES : (piece + 1) * LANES
            ].astype(BF16)
        if shard is not None:
            tail = turned[pieces * LANES :, to : to + count]
        else:
            tail = turned[pieces * LANES :, to : to + count]
            if first:
                kept = jnp.zeros((feature % LANES, first), F32)
                for other in range(shards):
                    start = other * SMALL + relay * POOL
                    part = turned[pieces * LANES :, start : start + first]
                    kept = jnp.where(busy == other, part, kept)
                tail = jnp.concatenate([kept, tail], axis=1)
        blank = jnp.zeros((tail.shape[0], LANES - tail.shape[1]), F32)
        out_ref[at, pieces * POOL :, :] = jnp.concatenate([tail, blank], axis=1).astype(BF16)


def edges_kernel(*refs, parts, pooled):
    refs = list(refs)
    src_ref, dst_ref, rel_ids_ref, rel_ref = refs[:4]
    neg_refs = refs[4 : 4 + parts]
    refs = refs[4 + parts :]
    if pooled:
        back_ref, src_slot_ref, dst_slot_ref, busy_ref = refs[:4]
        refs = refs[4:]
        pool_out_ref = refs.pop(2 + parts)
        pool_rows, pool_flat, pool_sums = refs[-3:]
    src_grad_ref, dst_grad_ref = refs[:2]
    neg_grad_refs = refs[2 : 2 + parts]
    negatives, rel_flat = refs[2 + parts : 4 + parts]
    block = pl.program_id(0)
    part = neg_refs[0].shape[1]

    @pl.when(block == 0)
    def _():
        table, pieces = rel_ref[...], []
        for _ in range(3):
            pieces.append(table.astype(BF16).astype(F32))
            table = table - pieces[-1]
        rel_flat[...] = jnp.concatenate(pieces, axis=0).T.astype(BF16)
        if pooled:
            compact_pool(back_ref, busy_ref[0, 0], pool_rows, pool_flat)
            pool_sums[...] = jnp.zeros(pool_sums.shape, F32)

    for k in range(parts):
        negatives[k * part : (k + 1) * part] = neg_refs[k][0]
    turned = negatives[...].astype(F32).T.astype(BF16)
    hot = one_hot(rel_ref.shape[0], rel_ids_ref[...].reshape(1, rel_ids_ref.shape[-1]))
    relation = dot(rel_flat[...], jnp.concatenate([hot] * 3, axis=0), NN)
    source = src_ref[...].astype(F32)
    target = dst_ref[...].astype(F32)
    if pooled:
        count = pool_flat.shape[1]
        src_hot = one_hot(count, src_slot_ref[...].reshape(1, src_slot_ref.shape[-1]))
        dst_hot = one_hot(count, dst_slot_ref[...].reshape(1, dst_slot_ref.shape[-1]))
        source = source + dot(pool_flat[...], src_hot, NN)
        target = target + dot(pool_flat[...], dst_hot, NN)
    product = source * relation
    positive = jnp.sum(product * target, axis=0, keepdims=True)
    pos_weight = -jax.nn.sigmoid(-positive)
    query = product.astype(BF16)
    weight = jax.nn.sigmoid(dot(negatives[...], query, NN)).astype(BF16)
    gathered = dot(turned, weight, NN)
    src_grad = (relation * (pos_weight * target + gathered)).astype(BF16)
    dst_grad = (pos_weight * product).astype(BF16)
    src_grad_ref[...] = src_grad
    dst_grad_ref[...] = dst_grad
    neg_grad = dot(weight, query, NT)
    if pooled:
        pool_sums[...] += dot(src_hot, src_grad, NT) + dot(dst_hot, dst_grad, NT)

    for k in range(parts):
        neg_grad_refs[k][0] = neg_grad[k * part : (k + 1) * part].astype(BF16)
    if pooled:

        @pl.when(block == pl.num_programs(0) - 1)
        def _():
            expand_pool(pool_sums[...], busy_ref[0, 0], pool_out_ref)


def edges(rows, rel_ids, relations, negatives, pool=None, pool_slot=None, busy=None):
    feature, endpoints = rows.shape
    parts = len(negatives)
    spans, part, _ = negatives[0].shape
    width = rel_ids.shape[1]
    edge_spec = pl.BlockSpec((feature, width), lambda b: (0, b))
    neg_spec = pl.BlockSpec((1, part, feature), lambda b: (b, 0, 0))
    operands = [rows, rows, rel_ids.reshape(spans, 1, width), relations, *negatives]
    specs = [
        edge_spec,
        pl.BlockSpec((feature, width), lambda b: (0, spans + b)),
        pl.BlockSpec((1, 1, width), lambda b: (b, 0, 0)),
        pl.BlockSpec(relations.shape, lambda b: (0, 0)),
    ] + [neg_spec] * parts
    out_specs = [edge_spec, edge_spec] + [neg_spec] * parts
    out_shape = [jax.ShapeDtypeStruct((feature, endpoints // 2), BF16)] * 2
    out_shape += [jax.ShapeDtypeStruct((spans, part, feature), BF16)] * parts
    scratch = [
        pltpu.VMEM((parts * part, feature), BF16),
        pltpu.VMEM((feature, 3 * relations.shape[0]), BF16),
    ]
    if pool is not None:
        slot = pool_slot.reshape(2 * spans, 1, width)
        pool_spec = pl.BlockSpec(pool.shape, lambda b: (0, 0, 0))
        operands += [pool, slot, slot, busy]
        specs += [
            pool_spec,
            pl.BlockSpec((1, 1, width), lambda b: (b, 0, 0)),
            pl.BlockSpec((1, 1, width), lambda b: (spans + b, 0, 0)),
            pl.BlockSpec(memory_space=pltpu.SMEM),
        ]
        out_specs.append(pool_spec)
        out_shape.append(jax.ShapeDtypeStruct(pool.shape, BF16))
        count = compact_size(pool.shape[0] // RELAYS)
        scratch += [
            pltpu.VMEM((count, feature // LANES * LANES), BF16),
            pltpu.VMEM((feature, count), BF16),
            pltpu.VMEM((count, feature), F32),
        ]
    src_grad, dst_grad, *rest = call(
        functools.partial(edges_kernel, parts=parts, pooled=pool is not None),
        "edges",
        6 * feature * parts * part * spans * width,
        4 * (rows.size + parts * negatives[0].size),
        grid=(spans,),
        in_specs=specs,
        out_specs=out_specs,
        out_shape=out_shape,
        scratch_shapes=scratch,
    )(*operands)
    return src_grad, dst_grad, rest


def collect_kernel(src_ref, dst_ref, slot_ref, out_ref, *, group):
    segments, width = slot_ref.shape
    feature = src_ref.shape[0]
    step = pl.program_id(0)
    total = jnp.zeros((feature, group * LANES), F32)
    for segment in range(segments):
        grads = src_ref if segment < segments // 2 else dst_ref
        start = segment % (segments // 2) * width
        hot = one_hot(group * LANES, slot_ref[segment : segment + 1, :], step * group * LANES)
        total = total + dot(grads[:, start : start + width], hot, NT)
    total = total.astype(BF16)
    first = out_ref.shape[1] - feature
    for i in range(group):
        out_ref[i, first:] = total[:, i * LANES : (i + 1) * LANES]


def collect(src_grad, dst_grad, slot, devices, neg_cap=0):
    feature = src_grad.shape[0]
    group = 4
    slots = devices * LANES
    height = feature + (packed_height(neg_cap, feature) if neg_cap else 0)
    whole = pl.BlockSpec(src_grad.shape, lambda i: (0, 0))
    return call(
        functools.partial(collect_kernel, group=group),
        "collect_grads",
        2 * feature * slots * slot.size,
        2 * feature * (slots + slot.size),
        grid=(devices // group,),
        in_specs=[whole, whole, pl.BlockSpec(slot.shape, lambda i: (0, 0))],
        out_specs=pl.BlockSpec((group, height, LANES), lambda i: (i, 0, 0)),
        out_shape=jax.ShapeDtypeStruct((devices, height, LANES), BF16),
    )(src_grad, dst_grad, slot)


def collect_neg_kernel(sent_ref, slot_ref, *refs, group, cap):
    grad_refs, out_ref, sums = refs[:-2], refs[-2], refs[-1]
    step = pl.program_id(0)

    @pl.when(step == 0)
    def _():
        total = grad_refs[0][...].astype(F32)
        for grad_ref in grad_refs[1:]:
            total = total + grad_ref[...].astype(F32)
        sums[...] = total.astype(BF16)

    rows = jnp.zeros((group * cap, sums.shape[-1]), F32)
    for part in range(slot_ref.shape[0]):
        hot = one_hot(group * cap, slot_ref[part : part + 1, :], step * group * cap)
        rows = rows + dot(hot, sums[part], NN)
    pack_all(out_ref, 0, cap, rows, rows.T)


def collect_neg(sent, slot, grads, cap):
    devices = sent.shape[0]
    feature = grads[0].shape[-1]
    group = 16
    height = packed_height(cap, feature)
    return call(
        functools.partial(collect_neg_kernel, group=group, cap=cap),
        "collect_negatives",
        2 * devices * cap * feature * slot.size,
        4 * len(grads) * grads[0].size,
        grid=(devices // group,),
        in_specs=[
            pl.BlockSpec(memory_space=pl.ANY),
            pl.BlockSpec(slot.shape, lambda i: (0, 0)),
        ]
        + [pl.BlockSpec(grads[0].shape, lambda i: (0, 0, 0))] * len(grads),
        out_specs=pl.BlockSpec((group, height, LANES), lambda i: (i, 0, 0)),
        out_shape=jax.ShapeDtypeStruct(sent.shape, BF16),
        scratch_shapes=[pltpu.VMEM(grads[0].shape, BF16)],
        input_output_aliases={0: 0},
    )(sent, slot, *grads)


def add_kernel(*refs, rows, neg_cap, first):
    refs = list(refs)
    recv_ref, req_ref = refs[:2]
    refs = refs[2:]
    if neg_cap:
        neg_req_ref = refs.pop(0)
        neg_rows, neg_flat = refs[-2:]
    if not first:
        so_far_ref = refs.pop(0)
    out_ref, flat = refs[:2]
    devices = recv_ref.shape[0]
    feature = flat.shape[0]
    step = pl.program_id(0)

    @pl.when(step == 0)
    def _():
        start = recv_ref.shape[1] - feature
        for d in range(devices):
            flat[:, d * LANES : (d + 1) * LANES] = recv_ref[d, start:]
        if neg_cap:
            unpack_all(recv_ref, 0, neg_cap, neg_rows, neg_flat)

    base = step * rows
    row = jnp.concatenate([req_ref[d : d + 1, :] for d in range(devices)], axis=1)
    total = dot(flat[...], one_hot(rows, row, base), NT)
    if neg_cap:
        row = jnp.concatenate([neg_req_ref[d : d + 1, :neg_cap] for d in range(devices)], axis=1)
        total = total + dot(neg_flat[...], one_hot(rows, row, base), NT)
    if not first:
        total = total + so_far_ref[...]
    out_ref[...] = total


def add_rows(recv, requests, so_far, feature, rows_dev, neg_requests=None, neg_cap=0):
    devices = recv.shape[0]
    rows = 512 if devices * LANES <= 4096 else 128
    slots = devices * LANES
    whole_req = pl.BlockSpec((devices, LANES), lambda i: (0, 0))
    rows_spec = pl.BlockSpec((feature, rows), lambda i: (0, i))
    operands = [recv, requests]
    specs = [pl.BlockSpec(recv.shape, lambda i: (0, 0, 0)), whole_req]
    scratch = [pltpu.VMEM((feature, slots), BF16)]
    if neg_cap:
        operands.append(neg_requests)
        specs.append(whole_req)
        scratch += unpack_scratch(devices, neg_cap, feature)
    if so_far is not None:
        operands.append(so_far)
        specs.append(rows_spec)
    return call(
        functools.partial(add_kernel, rows=rows, neg_cap=neg_cap, first=so_far is None),
        "add_grads",
        2 * feature * slots * rows_dev,
        2 * feature * slots + 8 * feature * rows_dev,
        grid=(rows_dev // rows,),
        in_specs=specs,
        out_specs=rows_spec,
        out_shape=jax.ShapeDtypeStruct((feature, rows_dev), F32),
        scratch_shapes=scratch,
    )(*operands)


def add_quarters_kernel(
    recv_ref, req_ref, neg_req_ref, so_far_ref, out_ref, flat, neg_rows, neg_flat, *, neg_cap
):
    devices = recv_ref.shape[0]
    feature, rows = out_ref.shape
    step = pl.program_id(0)

    @pl.when(step == 0)
    def _():
        start = recv_ref.shape[1] - feature
        for first in range(0, devices, PARTS):
            for part in range(PARTS):
                for j in range(PARTS):
                    to = first // PARTS * LANES + j * SHARE
                    flat[part, :, to : to + SHARE] = recv_ref[
                        first + (part ^ j), start:, j * SHARE : (j + 1) * SHARE
                    ]
        unpack_all(recv_ref, 0, neg_cap, neg_rows, neg_flat)

    base = step * rows
    asked = quarter_ids([req_ref[d : d + 1, :] for d in range(devices)])
    row = asked[0]
    for part in range(1, PARTS):
        row = jnp.where(step == part, asked[part], row)
    total = dot(flat[step], one_hot(rows, row, base), NT)
    row = jnp.concatenate([neg_req_ref[d : d + 1, :neg_cap] for d in range(devices)], axis=1)
    out_ref[...] = total + dot(neg_flat[...], one_hot(rows, row, base), NT) + so_far_ref[...]


def add_quarters(recv, requests, neg_requests, so_far, neg_cap):
    feature, rows_dev = so_far.shape
    devices = recv.shape[0]
    slots = devices * LANES
    whole_req = pl.BlockSpec((devices, LANES), lambda i: (0, 0))
    rows_spec = pl.BlockSpec((feature, rows_dev // PARTS), lambda i: (0, i))
    return call(
        functools.partial(add_quarters_kernel, neg_cap=neg_cap),
        "add_quarters",
        feature * (slots // 2 + 2 * devices * neg_cap) * rows_dev,
        2 * feature * slots + 8 * feature * rows_dev,
        grid=(PARTS,),
        in_specs=[pl.BlockSpec(recv.shape, lambda i: (0, 0, 0)), whole_req, whole_req, rows_spec],
        out_specs=rows_spec,
        out_shape=jax.ShapeDtypeStruct((feature, rows_dev), F32),
        scratch_shapes=[pltpu.VMEM((PARTS, feature, slots // PARTS), BF16)]
        + unpack_scratch(devices, neg_cap, feature),
    )(recv, requests, neg_requests, so_far)


def add_pool_kernel(*refs, rows, first):
    one_ref, two_ref, one_req_ref, two_req_ref = refs[:4]
    out_ref, packed, *flats = refs[4 + (not first) :]
    step = pl.program_id(0)

    @pl.when(step == 0)
    def _():
        for recv_ref, flat in zip((one_ref, two_ref), flats):
            unpack_all(recv_ref, 0, POOL, packed, flat)

    total = dot(flats[0][...], one_hot(rows, one_req_ref[...], step * rows), NT)
    total = total + dot(flats[1][...], one_hot(rows, two_req_ref[...], step * rows), NT)
    if not first:
        total = total + refs[4][...]
    out_ref[...] = total


def add_pool(one, two, requests, so_far, feature, rows_dev):
    rows = 512
    devices = one.shape[0]
    slots = devices * POOL
    recv_spec = pl.BlockSpec(one.shape, lambda i: (0, 0, 0))
    req_spec = pl.BlockSpec((1, slots), lambda i: (0, 0))
    rows_spec = pl.BlockSpec((feature, rows), lambda i: (0, i))
    packed, flat = unpack_scratch(devices, POOL, feature)
    extra = [] if so_far is None else [so_far]
    return call(
        functools.partial(add_pool_kernel, rows=rows, first=so_far is None),
        "add_pool",
        4 * feature * slots * rows_dev,
        4 * feature * slots + 4 * feature * rows_dev,
        grid=(rows_dev // rows,),
        in_specs=[recv_spec, recv_spec, req_spec, req_spec] + [rows_spec] * len(extra),
        out_specs=rows_spec,
        out_shape=jax.ShapeDtypeStruct((feature, rows_dev), F32),
        scratch_shapes=[packed, flat, flat],
    )(one, two, requests[0][None], requests[1][None], *extra)


def after(value, other):
    anywhere = pl.BlockSpec(memory_space=pl.ANY)
    return call(
        lambda value_ref, other_ref, out_ref: None,
        "after",
        0,
        0,
        in_specs=[anywhere, anywhere],
        out_specs=anywhere,
        out_shape=jax.ShapeDtypeStruct(value.shape, value.dtype),
        input_output_aliases={0: 0},
    )(value, other)


def exchange(value):
    return lax.all_to_all(value, ("shard", "grp"), split_axis=0, concat_axis=0, tiled=True)


def swap(value, bit):
    sharers = lax.axis_size("grp")
    return lax.ppermute(value, "grp", [(i, i ^ bit) for i in range(sharers)])


def share_out(value, wait=lambda block: block):
    sharers = lax.axis_size("grp")
    blocks = {0: value}
    bit = sharers // 2
    while bit:
        for k in list(blocks):
            blocks[k ^ bit] = swap(wait(blocks[k]) if k else blocks[k], bit)
        bit //= 2
    return [blocks[k] for k in range(sharers)]


def trade(blocks):
    sharers = len(blocks)
    terms = [[block] for block in blocks]
    bit = 1
    while bit < sharers:
        for k in range(0, sharers, 2 * bit):
            total = terms[k ^ bit][0].astype(F32)
            for term in terms[k ^ bit][1:]:
                total = total + term.astype(F32)
            terms[k].append(swap(total.astype(BF16), bit))
        bit *= 2
    return terms[0]


def pad_lanes(value, width, fill):
    return jnp.pad(value, ((0, 0), (0, width - value.shape[1])), constant_values=fill)


def body(entity_table, rel_diag, src_ids, dst_ids, rel_ids, neg_ids):
    rows_dev, feature = entity_table.shape
    sharers = lax.axis_size("grp")
    devices = lax.axis_size("shard") * sharers
    spans, neg_count = neg_ids.shape
    edge_count = src_ids.shape[0]
    block_len = edge_count // spans
    edge_cap = 4 * edge_count // devices
    chunks = round_up(edge_cap, LANES) // LANES
    part_width = neg_count // sharers
    neg_cap = round_up(2 * spans * part_width // devices, 16)
    width = round_up(block_len, 512)
    part = round_up(part_width, LANES)
    me = lax.axis_index("grp")

    table = entity_table.T.astype(BF16)
    own_ids = lax.dynamic_slice_in_dim(neg_ids, me * part_width, part_width, 1)
    rel_rows = pad_lanes(rel_ids.reshape(spans, block_len), width, -1)

    def ask(zero, chunks):
        message, *slots = make_slots(
            lax.axis_index(("shard", "grp")),
            src_ids + zero,
            dst_ids + zero,
            own_ids,
            rows_dev,
            devices,
            chunks,
            neg_cap,
            width,
            part,
        )
        asked = exchange(message)
        return asked, asked[:, -LANES:], slots, slots[-1]

    def chunked(zero):
        asked, neg_asked, slots, neg_slot = ask(zero, chunks)
        direct = [asked[:, c * LANES : (c + 1) * LANES] for c in range(chunks)]
        back = [exchange(gather(table, direct[0], neg_asked, neg_cap))]
        back += [exchange(gather(table, direct[c])) for c in range(1, chunks)]
        negatives = share_out(spread_neg(back[0], neg_slot, neg_cap, feature))
        rows = None
        for c in range(chunks):
            rows = spread(back[c], slots[c], rows, feature)
        src_grad, dst_grad, neg_grads = edges(rows, rel_rows, rel_diag, negatives)
        grad = None
        for c in range(1, chunks):
            sent = exchange(collect(src_grad, dst_grad, slots[c], devices))
            grad = add_rows(sent, direct[c], grad, feature, rows_dev)
        sent = collect(src_grad, dst_grad, slots[0], devices, neg_cap)
        sent = exchange(collect_neg(sent, neg_slot, trade(neg_grads), neg_cap))
        return add_rows(sent, direct[0], grad, feature, rows_dev, neg_asked, neg_cap)

    def pooled():
        asked, neg_asked, (slot, pool_slot, busy, _), neg_slot = ask(0, 0)
        direct = asked[:, :LANES]
        listed = asked[:, LANES : LANES + RELAYS * POOL].reshape(devices, RELAYS, POOL)
        listed = listed.transpose(1, 0, 2).reshape(RELAYS, devices * POOL) - me * rows_dev
        listed = listed[me ^ jnp.arange(RELAYS, dtype=jnp.int32)]
        back = exchange(gather_quarters(table, direct, neg_asked, neg_cap))
        far = swap(gather_pool(table, listed[3], devices), 1)
        far = swap(gather_pool(table, listed[2], devices) + far, 2)
        near = swap(gather_pool(table, listed[1], devices), 1)
        near = gather_pool(table, listed[0], devices) + near
        rows = spread(back, slot, None, feature)
        negatives = share_out(
            spread_neg(back, neg_slot, neg_cap, feature), lambda block: after(block, rows)
        )
        src_grad, dst_grad, rest = edges(
            rows, rel_rows, rel_diag, negatives, exchange(near + far), pool_slot, busy
        )
        neg_grads, pool = rest[:-1], rest[-1]
        near = exchange(pool)
        far = swap(near, 2)
        sent = collect(src_grad, dst_grad, slot, devices, neg_cap)
        sent = exchange(collect_neg(sent, neg_slot, trade(neg_grads), neg_cap))
        grad = add_pool(near, swap(near, 1), listed[:2], None, feature, rows_dev)
        far = after(far, grad)
        grad = add_pool(far, swap(far, 1), listed[2:], grad, feature, rows_dev)
        return add_quarters(sent, direct, neg_asked, grad, neg_cap), jnp.max(neg_asked[:, -1])

    if chunks == 1 or sharers != RELAYS:
        return chunked(0).T
    return lax.while_loop(
        lambda state: state[1] > 0,
        lambda state: (chunked(jnp.minimum(state[1], 0)), -state[1]),
        pooled(),
    )[0].T


def solution(mesh):
    placed = (
        P(("shard", "grp"), None),
        P(),
        P(("shard", "grp")),
        P(("shard", "grp")),
        P(("shard", "grp")),
        P("shard", None),
    )
    return jax.shard_map(
        body, mesh=mesh, in_specs=placed, out_specs=P(("shard", "grp"), None), check_vma=False
    )
```

profile of v0, /device:TPU:0, one launch (start us, length us, event | category | flops | bytes accessed | tf_op | source)
XLA Modules:
  0.0 341.5 jit_solution(16636142345088251110)
XLA Ops:
  0.0 0.7 copy-done
  0.8 3.9 %slots.2 = (s32[32,512]{1,0:T(8,128)}, s32[4,1024]{1,0:T(4,128)}, s32[4,1024]{1,0:T(4,128)}, s32[1,1]{1,0:T(1,128)}, s32[2,256]{1,0:T(2,128)}) custom-call(s32[1,1]{1,0:T(1,128)} %bitcast.3.me_ref, s32[2000]{0:T(1024)} %src_ref.1, s32[2000]{0:T(1024)} %dst_ref.1, s32[2,250]{1,0:T(2,128)S(1)} %constant_dynamic-slice_fusion.own_ref), custom_call_target="tpu_custom_call" | custom-call | flops 268435456 | bytes 32768 | tf_op jit(solution)/shard_map/slots/pallas_call | solution.py:179
  4.6 1.5 copy.17
  6.2 7.3 %all-to-all-start.5 = ((s32[32,1,512]{2,1,0:T(1,128)}), s32[32,1,512]{2,1,0:T(1,128)S(1)}, u32[]{:S(2)}, u32[]{:S(2)}) async-start(s32[32,1,512]{2,1,0:T(1,128)} %copy.17), calls=%async_computation.5 | async-start | bytes 131072 | tf_op jit(solution)/shard_map/all_to_all | solution.py:860
  13.5 3.3 convert_bitcast_fusion.table_ref
  16.8 4.1 %all-to-all-done.5 = s32[32,1,512]{2,1,0:T(1,128)S(1)} async-done(((s32[32,1,512]{2,1,0:T(1,128)}), s32[32,1,512]{2,1,0:T(1,128)S(1)}, u32[]{:S(2)}, u32[]{:S(2)}) %all-to-all-start.5) | async-done | bytes 65568 | tf_op jit(solution)/shard_map/all_to_all | solution.py:860
  20.9 0.6 fusion.2
  21.5 11.5 %gather_quarters.1 = bf16[32,512,128]{2,1,0:T(8,128)(2,1)} custom-call(bf16[400,4096]{1,0:T(8,128)(2,1)S(1)} %convert_bitcast_fusion.table_ref, s32[32,128]{1,0:T(8,128)} %get-tuple-element.103.req_ref, s32[32,128]{1,0:T(8,128)} %get-tuple-element.102.neg_req_ref), custom_call_target="tpu_custom_call" | custom-call | flops 6710886400 | bytes 7372800 | tf_op jit(solution)/shard_map/gather_quarters/pallas_call | solution.py:330
  33.0 4.1 %all-to-all-start.6 = ((bf16[32,512,128]{2,1,0:T(8,128)(2,1)}), bf16[32,512,128]{2,1,0:T(8,128)(2,1)}, u32[]{:S(2)}, u32[]{:S(2)}) async-start(bf16[32,512,128]{2,1,0:T(8,128)(2,1)} %gather_quarters.1), calls=%async_computation.6 | async-start | bytes 8388608 | tf_op jit(solution)/shard_map/all_to_all | solution.py:860
  37.2 0.1 sub.17
  37.3 0.1 sub.19
  37.4 0.6 gather_fusion
  38.0 0.6 fusion.3
  38.6 9.3 %gather_pool.7 = bf16[32,160,128]{2,1,0:T(8,128)(2,1)} custom-call(bf16[400,4096]{1,0:T(8,128)(2,1)S(1)} %convert_bitcast_fusion.table_ref, s32[4,1,384]{2,1,0:T(1,128)} %bitcast.37), custom_call_target="tpu_custom_call" | custom-call | flops 5033164800 | bytes 4505600 | tf_op jit(solution)/shard_map/gather_pool/pallas_call | solution.py:354
  47.9 0.2 collective-permute-start.10
  48.1 9.3 %gather_pool.5 = bf16[32,160,128]{2,1,0:T(8,128)(2,1)} custom-call(bf16[400,4096]{1,0:T(8,128)(2,1)S(1)} %convert_bitcast_fusion.table_ref, s32[4,1,384]{2,1,0:T(1,128)} %bitcast.38), custom_call_target="tpu_custom_call" | custom-call | flops 5033164800 | bytes 4505600 | tf_op jit(solution)/shard_map/gather_pool/pallas_call | solution.py:354
  57.4 0.3 collective-permute-start.9
  57.7 9.3 %gather_pool.6 = bf16[32,160,128]{2,1,0:T(8,128)(2,1)} custom-call(bf16[400,4096]{1,0:T(8,128)(2,1)S(1)} %convert_bitcast_fusion.table_ref, s32[4,1,384]{2,1,0:T(1,128)} %bitcast.36), custom_call_target="tpu_custom_call" | custom-call | flops 5033164800 | bytes 4505600 | tf_op jit(solution)/shard_map/gather_pool/pallas_call | solution.py:354
  67.0 1.7 add.50
  68.7 1.8 collective-permute-start.11
  70.5 9.3 %gather_pool.4 = bf16[32,160,128]{2,1,0:T(8,128)(2,1)} custom-call(bf16[400,4096]{1,0:T(8,128)(2,1)S(1)} %convert_bitcast_fusion.table_ref, s32[4,1,384]{2,1,0:T(1,128)} %bitcast.39), custom_call_target="tpu_custom_call" | custom-call | flops 5033164800 | bytes 4505600 | tf_op jit(solution)/shard_map/gather_pool/pallas_call | solution.py:354
  79.8 32.7 %collective-permute-done.11 = bf16[32,160,128]{2,1,0:T(8,128)(2,1)S(1)} collective-permute-done((bf16[32,160,128]{2,1,0:T(8,128)(2,1)S(1)}, bf16[32,160,128]{2,1,0:T(8,128)(2,1)S(1)}, u32[]{:S(2)}, u32[]{:S(2)}) %collective-permute-start.11) | collective-permute-done | bytes 1310752 | tf_op jit(solution)/shard_map/ppermute | solution.py:865
  112.5 2.7 add_add_fusion
  115.2 16.1 %all-to-all-done.6.refs_0_.back_ref = bf16[32,512,128]{2,1,0:T(8,128)(2,1)} async-done(((bf16[32,512,128]{2,1,0:T(8,128)(2,1)}), bf16[32,512,128]{2,1,0:T(8,128)(2,1)}, u32[]{:S(2)}, u32[]{:S(2)}) %all-to-all-start.6) | async-done | bytes 4194336 | tf_op jit(solution)/shard_map/all_to_all | solution.py:860
  131.3 4.0 %all-to-all-start.7 = ((bf16[32,160,128]{2,1,0:T(8,128)(2,1)}), bf16[32,160,128]{2,1,0:T(8,128)(2,1)}, u32[]{:S(2)}, u32[]{:S(2)}) async-start(bf16[32,160,128]{2,1,0:T(8,128)(2,1)} %add_add_fusion), calls=%async_computation.7 | async-start | bytes 2621440 | tf_op jit(solution)/shard_map/all_to_all | solution.py:860
  135.3 0.6 reshape.54.refs_1_
  135.9 2.9 spread_negatives.2.refs_4_
  138.8 1.9 collective-permute-start.7
  140.7 19.3 %spread_rows.3.other_ref.refs_0_.refs_1_ = bf16[400,4096]{1,0:T(8,128)(2,1)} custom-call(bf16[32,512,128]{2,1,0:T(8,128)(2,1)} %all-to-all-done.6.refs_0_.back_ref, s32[4,1,1024]{2,1,0:T(1,128)} %reshape.54.refs_1_), custom_call_target="tpu_custom_call" | custom-call | flops 13421772800 | bytes 6553600 | tf_op jit(solution)/shard_map/spread_rows/pallas_call | solution.py:424
  160.0 1.6 collective-permute-done.7.refs_6_
  161.5 0.8 copy-done.9
  162.4 0.8 copy.36.value_ref
  163.2 0.2 collective-permute-start.8
  163.5 0.6 reshape.56.refs_2_
  164.1 0.6 reshape.57.refs_9_.refs_10_
  164.7 2.8 all-to-all-done.7.refs_8_
  167.5 20.2 %edges.2 = (bf16[400,2048]{1,0:T(8,128)(2,1)}, bf16[400,2048]{1,0:T(8,128)(2,1)}, bf16[2,256,400]{2,1,0:T(8,128)(2,1)}, bf16[2,256,400]{2,1,0:T(8,128)(2,1)}, bf...) custom-call(bf16[400,4096]{1,0:T(8,128)(2,1)} %spread_rows.3.other_ref.refs_0_.refs_1_, ...), custom_call_target="tpu_custom_call" | custom-call | flops 5033164800 | bytes 9830400 | tf_op jit(solution)/shard_map/edges/pallas_call | solution.py:606
  187.8 4.1 %all-to-all-start.9 = ((bf16[32,160,128]{2,1,0:T(8,128)(2,1)}), bf16[32,160,128]{2,1,0:T(8,128)(2,1)}, u32[]{:S(2)}, u32[]{:S(2)}) async-start(bf16[32,160,128]{2,1,0:T(8,128)(2,1)} %get-tuple-element.79), calls=%async_computation.9 | async-start | bytes 2621440 | tf_op jit(solution)/shard_map/all_to_all | solution.py:860
  191.9 0.3 collective-permute-start.13
  192.1 0.3 collective-permute-start.12
  192.5 1.6 collective-permute-done.13
  194.1 1.2 add_convert_fusion.1
  195.2 1.8 collective-permute-start.14
  197.0 18.0 %collect_grads.3.sent_ref = bf16[32,512,128]{2,1,0:T(8,128)(2,1)} custom-call(bf16[400,2048]{1,0:T(8,128)(2,1)} %get-tuple-element.73.src_ref, bf16[400,2048]{1,0:T(8,128)(2,1)} %get-tuple-element.74.dst_ref, s32[4,1024]{1,0:T(4,128)} %get-tuple-element.69.slot_ref), custom_call_target="tpu_custom_call" | custom-call | flops 13421772800 | bytes 6553600 | tf_op jit(solution)/shard_map/collect_grads/pallas_call | solution.py:642
  215.0 3.1 collective-permute-done.14.refs_2_
  218.2 0.8 copy-done.11
  218.9 3.5 %collect_negatives.2 = bf16[32,512,128]{2,1,0:T(8,128)(2,1)} custom-call(bf16[32,512,128]{2,1,0:T(8,128)(2,1)} %collect_grads.3.sent_ref, s32[2,256]{1,0:T(2,128)} %get-tuple-element.70.slot_ref, bf16[2,256,400]{2,1,0:T(8,128)(2,1)} %get-tuple-element.75.refs_0_, bf16[2,256,400]{2,1,0:T(8,128)(2,1)} %copy-done.10, ...), custom_call_target="tpu_custom_call", output_to_operand_aliasing={{}: (0, {})} | custom-call | flops 419430400 | bytes 2457600 | tf_op jit(solution)/shard_map/collect_negatives/pallas_call | solution.py:677
  222.5 1.6 all-to-all-done.9.refs_0_
  224.1 4.9 %all-to-all-start.8 = ((bf16[32,512,128]{2,1,0:T(8,128)(2,1)}), bf16[32,512,128]{2,1,0:T(8,128)(2,1)}, u32[]{:S(2)}, u32[]{:S(2)}) async-start(bf16[32,512,128]{2,1,0:T(8,128)(2,1)} %collect_negatives.2), calls=%async_computation.8 | async-start | bytes 8388608 | tf_op jit(solution)/shard_map/all_to_all | solution.py:860
  229.0 0.4 collective-permute-start.16
  229.4 1.7 collective-permute-start.15
  231.1 1.2 collective-permute-done.16.refs_1_
  232.3 1.1 copy-done.21
  233.4 15.5 %add_pool.2.other_ref.refs_4_ = f32[400,4096]{1,0:T(8,128)} custom-call(bf16[32,160,128]{2,1,0:T(8,128)(2,1)} %all-to-all-done.9.refs_0_, bf16[32,160,128]{2,1,0:T(8,128)(2,1)} %copy-done.21, s32[1,1536]{1,0:T(1,128)} %get-tuple-element.106.refs_2_, s32[1,1536]{1,0:T(1,128)} %get-tuple-element.104.refs_3_), custom_call_target="tpu_custom_call" | custom-call | flops 10066329600 | bytes 9011200 | tf_op jit(solution)/shard_map/add_pool/pallas_call | solution.py:832
  248.9 50.2 %collective-permute-done.15.value_ref = bf16[32,160,128]{2,1,0:T(8,128)(2,1)S(1)} collective-permute-done((bf16[32,160,128]{2,1,0:T(8,128)(2,1)}, bf16[32,160,128]{2,1,0:T(8,128)(2,1)S(1)}, u32[]{:S(2)}, u32[]{:S(2)}) %collective-permute-start.15) | collective-permute-done | bytes 1310752 | tf_op jit(solution)/shard_map/ppermute | solution.py:865
  299.1 1.1 copy-done.8
  300.2 0.7 slice_reduce_fusion
  300.9 2.5 collective-permute-done.17.refs_1_
  303.5 1.1 copy-done.20
  304.5 16.0 %add_pool.3.so_far_ref = f32[400,4096]{1,0:T(8,128)} custom-call(bf16[32,160,128]{2,1,0:T(8,128)(2,1)} %after.3.refs_0_, bf16[32,160,128]{2,1,0:T(8,128)(2,1)} %copy-done.20, s32[1,1536]{1,0:T(1,128)} %get-tuple-element.105.refs_2_, s32[1,1536]{1,0:T(1,128)} %get-tuple-element.107.refs_3_, f32[400,4096]{1,0:T(8,128)} %add_pool.2.other_ref.refs_4_), custom_call_target="tpu_custom_call" | custom-call | flops 10066329600 | bytes 9011200 | tf_op jit(solution)/shard_map/add_pool/pallas_call | solution.py:832
  320.5 2.6 all-to-all-done.8.recv_ref
  323.2 15.6 %add_quarters.1 = f32[400,4096]{1,0:T(8,128)} custom-call(bf16[32,512,128]{2,1,0:T(8,128)(2,1)} %all-to-all-done.8.recv_ref, s32[32,128]{1,0:T(8,128)} %get-tuple-element.103.req_ref, s32[32,128]{1,0:T(8,128)} %get-tuple-element.102.neg_req_ref, f32[400,4096]{1,0:T(8,128)} %add_pool.3.so_far_ref), custom_call_target="tpu_custom_call" | custom-call | flops 6710886400 | bytes 16384000 | tf_op jit(solution)/shard_map/add_quarters/pallas_call | solution.py:792
  338.8 1.6 while.11
  340.4 0.7 copy-done.1
  (41 shorter events, 0.3 us)
Async XLA Ops:
  0.0 0.7 copy-start
  6.2 14.7 %all-to-all-start.5 = ((s32[32,1,512]{2,1,0:T(1,128)}), s32[32,1,512]{2,1,0:T(1,128)S(1)}, u32[]{:S(2)}, u32[]{:S(2)}) async-start(s32[32,1,512]{2,1,0:T(1,128)} %copy.17), calls=%async_computation.5 | async-start | bytes 131072 | tf_op jit(solution)/shard_map/all_to_all | solution.py:860
  33.0 98.3 %all-to-all-start.6 = ((bf16[32,512,128]{2,1,0:T(8,128)(2,1)}), bf16[32,512,128]{2,1,0:T(8,128)(2,1)}, u32[]{:S(2)}, u32[]{:S(2)}) async-start(bf16[32,512,128]{2,1,0:T(8,128)(2,1)} %gather_quarters.1), calls=%async_computation.6 | async-start | bytes 8388608 | tf_op jit(solution)/shard_map/all_to_all | solution.py:860
  47.9 19.1 %collective-permute-start.10 = (bf16[32,160,128]{2,1,0:T(8,128)(2,1)}, bf16[32,160,128]{2,1,0:T(8,128)(2,1)S(1)}, u32[]{:S(2)}, u32[]{:S(2)}) collective-permute-start(bf16[32,160,128]{2,1,0:T(8,128)(2,1)} %gather_pool.7), channel_id=1, source_target_pairs={{0,1},{1,0},{2,3},{3,2},{4,5},{5,4},{6,7},{7,6},{8,9},{9,8},{10,11... | collective-permute-start | bytes 3932168 | tf_op jit(solution)/shard_map/ppermute | solution.py:865
  57.4 22.4 %collective-permute-start.9 = (bf16[32,160,128]{2,1,0:T(8,128)(2,1)}, bf16[32,160,128]{2,1,0:T(8,128)(2,1)S(1)}, u32[]{:S(2)}, u32[]{:S(2)}) collective-permute-start(bf16[32,160,128]{2,1,0:T(8,128)(2,1)} %gather_pool.5), channel_id=1, source_target_pairs={{0,1},{1,0},{2,3},{3,2},{4,5},{5,4},{6,7},{7,6},{8,9},{9,8},{10,11... | collective-permute-start | bytes 3932168 | tf_op jit(solution)/shard_map/ppermute | solution.py:865
  68.7 43.7 %collective-permute-start.11 = (bf16[32,160,128]{2,1,0:T(8,128)(2,1)S(1)}, bf16[32,160,128]{2,1,0:T(8,128)(2,1)S(1)}, u32[]{:S(2)}, u32[]{:S(2)}) collective-permute-start(bf16[32,160,128]{2,1,0:T(8,128)(2,1)S(1)} %add.50), channel_id=1, source_target_pairs={{0,2},{1,3},{2,0},{3,1},{4,6},{5,7},{6,4},{7,5},{8,10},{9,11},{10,... | collective-permute-start | bytes 3932168 | tf_op jit(solution)/shard_map/ppermute | solution.py:865
  79.8 55.5 %copy-start.17 = (s32[4,1024]{1,0:T(4,128)S(1)}, s32[4,1024]{1,0:T(4,128)}, u32[]{:S(2)}) copy-start(s32[4,1024]{1,0:T(4,128)} %get-tuple-element.69.slot_ref) | copy-start | bytes 49156
  131.3 36.2 %all-to-all-start.7 = ((bf16[32,160,128]{2,1,0:T(8,128)(2,1)}), bf16[32,160,128]{2,1,0:T(8,128)(2,1)}, u32[]{:S(2)}, u32[]{:S(2)}) async-start(bf16[32,160,128]{2,1,0:T(8,128)(2,1)} %add_add_fusion), calls=%async_computation.7 | async-start | bytes 2621440 | tf_op jit(solution)/shard_map/all_to_all | solution.py:860
  138.8 22.7 %collective-permute-start.7 = (bf16[2,256,400]{2,1,0:T(8,128)(2,1)}, bf16[2,256,400]{2,1,0:T(8,128)(2,1)S(1)}, u32[]{:S(2)}, u32[]{:S(2)}) collective-permute-start(bf16[2,256,400]{2,1,0:T(8,128)(2,1)} %spread_negatives.2.refs_4_), channel_id=1, source_target_pairs={{0,2},{1,3},{2,0},{3,1},{4,6},{5,7},{6,4},{7,5},{8,10},{9,11},{10,... | collective-permute-start | bytes 1228808 | tf_op jit(solution)/shard_map/ppermute | solution.py:865
  140.7 26.8 %collective-permute-start.6 = (bf16[2,256,400]{2,1,0:T(8,128)(2,1)}, bf16[2,256,400]{2,1,0:T(8,128)(2,1)}, u32[]{:S(2)}, u32[]{:S(2)}) collective-permute-start(bf16[2,256,400]{2,1,0:T(8,128)(2,1)} %spread_negatives.2.refs_4_), channel_id=1, source_target_pairs={{0,1},{1,0},{2,3},{3,2},{4,5},{5,4},{6,7},{7,6},{8,9},{9,8},{10,11... | collective-permute-start | bytes 1228808 | tf_op jit(solution)/shard_map/ppermute | solution.py:865
  160.0 3.4 %copy-start.19 = (s32[2000]{0:T(1024)S(1)}, s32[2000]{0:T(1024)}, u32[]{:S(2)}) copy-start(s32[2000]{0:T(1024)} %param.12) | copy-start | bytes 24004
  160.0 4.1 %copy-start.18 = (s32[4,1024]{1,0:T(4,128)S(1)}, s32[4,1024]{1,0:T(4,128)}, u32[]{:S(2)}) copy-start(s32[4,1024]{1,0:T(4,128)} %get-tuple-element.71) | copy-start | bytes 49156
  160.0 7.5 %copy-start.22 = (f32[64,400]{1,0:T(8,128)S(1)}, f32[64,400]{1,0:T(8,128)}, u32[]{:S(2)}) copy-start(f32[64,400]{1,0:T(8,128)} %refs_3_.1) | copy-start | bytes 307204
  161.5 0.8 copy-start.9
  163.2 4.3 %collective-permute-start.8 = (bf16[2,256,400]{2,1,0:T(8,128)(2,1)}, bf16[2,256,400]{2,1,0:T(8,128)(2,1)}, u32[]{:S(2)}, u32[]{:S(2)}) collective-permute-start(bf16[2,256,400]{2,1,0:T(8,128)(2,1)} %after.2), channel_id=1, source_target_pairs={{0,1},{1,0},{2,3},{3,2},{4,5},{5,4},{6,7},{7,6},{8,9},{9,8},{10,11... | collective-permute-start | bytes 1228808 | tf_op jit(solution)/shard_map/ppermute | solution.py:865
  163.5 136.7 %copy-start.16 = (s32[2,1024]{1,0:T(2,128)}, s32[2,1024]{1,0:T(2,128)S(1)}, u32[]{:S(2)}) copy-start(s32[2,1024]{1,0:T(2,128)S(1)} %pad.4) | copy-start | bytes 24580
  187.8 36.3 %all-to-all-start.9 = ((bf16[32,160,128]{2,1,0:T(8,128)(2,1)}), bf16[32,160,128]{2,1,0:T(8,128)(2,1)}, u32[]{:S(2)}, u32[]{:S(2)}) async-start(bf16[32,160,128]{2,1,0:T(8,128)(2,1)} %get-tuple-element.79), calls=%async_computation.9 | async-start | bytes 2621440 | tf_op jit(solution)/shard_map/all_to_all | solution.py:860
  191.9 2.2 collective-permute-start.13
  192.1 22.9 %collective-permute-start.12 = (bf16[2,256,400]{2,1,0:T(8,128)(2,1)}, bf16[2,256,400]{2,1,0:T(8,128)(2,1)S(1)}, u32[]{:S(2)}, u32[]{:S(2)}) collective-permute-start(bf16[2,256,400]{2,1,0:T(8,128)(2,1)} %get-tuple-element.76), channel_id=1, source_target_pairs={{0,1},{1,0},{2,3},{3,2},{4,5},{5,4},{6,7},{7,6},{8,9},{9,8},{10,11... | collective-permute-start | bytes 1228808 | tf_op jit(solution)/shard_map/ppermute | solution.py:865
  195.2 22.9 %collective-permute-start.14 = (bf16[2,256,400]{2,1,0:T(8,128)(2,1)S(1)}, bf16[2,256,400]{2,1,0:T(8,128)(2,1)S(1)}, u32[]{:S(2)}, u32[]{:S(2)}) collective-permute-start(bf16[2,256,400]{2,1,0:T(8,128)(2,1)S(1)} %add_convert_fusion.1), channel_id=1, source_target_pairs={{0,2},{1,3},{2,0},{3,1},{4,6},{5,7},{6,4},{7,5},{8,10},{9,11},{10,... | collective-permute-start | bytes 1228808 | tf_op jit(solution)/shard_map/ppermute | solution.py:865
  215.0 3.1 copy-start.10
  218.2 0.8 copy-start.11
  224.1 99.0 %all-to-all-start.8 = ((bf16[32,512,128]{2,1,0:T(8,128)(2,1)}), bf16[32,512,128]{2,1,0:T(8,128)(2,1)}, u32[]{:S(2)}, u32[]{:S(2)}) async-start(bf16[32,512,128]{2,1,0:T(8,128)(2,1)} %collect_negatives.2), calls=%async_computation.8 | async-start | bytes 8388608 | tf_op jit(solution)/shard_map/all_to_all | solution.py:860
  229.0 3.3 collective-permute-start.16
  229.4 69.7 %collective-permute-start.15 = (bf16[32,160,128]{2,1,0:T(8,128)(2,1)}, bf16[32,160,128]{2,1,0:T(8,128)(2,1)S(1)}, u32[]{:S(2)}, u32[]{:S(2)}) collective-permute-start(bf16[32,160,128]{2,1,0:T(8,128)(2,1)} %all-to-all-done.9.refs_0_), channel_id=1, source_target_pairs={{0,2},{1,3},{2,0},{3,1},{4,6},{5,7},{6,4},{7,5},{8,10},{9,11},{10,... | collective-permute-start | bytes 3932168 | tf_op jit(solution)/shard_map/ppermute | solution.py:865
  232.3 1.1 copy-start.21
  299.1 1.1 copy-start.8
  300.2 3.2 collective-permute-start.17
  303.5 1.1 copy-start.20
  320.5 18.2 %copy-start.14 = (s32[2000]{0:T(1024)S(1)}, s32[2000]{0:T(1024)}, u32[]{:S(2)}) copy-start(s32[2000]{0:T(1024)} %src_ref.1) | copy-start | bytes 24004
  320.5 18.2 %copy-start.15 = (s32[2000]{0:T(1024)S(1)}, s32[2000]{0:T(1024)}, u32[]{:S(2)}) copy-start(s32[2000]{0:T(1024)} %dst_ref.1) | copy-start | bytes 24004
  340.4 0.7 copy-start.1
where the time goes:
time: 348 us; the launch traced here: 341 us
  Pallas kernels  164 us (47%)
  waiting for transfers between devices  120 us (34%)
  starting transfers between devices  33.2 us (10%)
  local copies, waits for them, and re-layouts  12.6 us (4%)
  other arithmetic  9.7 us (3%)
    ppermute x12, waiting for transfers between devices, swap(): return lax.ppermute(value, 'grp', [(i, i ^ bit) for i in range(sharers)])  92.9 us
    pallas_call x4, Pallas kernels, gather_pool(): call(functools.partial(gather_pool_kernel, group=group), 'gather_pool', 2...  37.1 us
    pallas_call x2, Pallas kernels, add_pool(): call(functools.partial(add_pool_kernel, rows=rows, first=so_far is None),...  31.5 us
    all_to_all x5, waiting for transfers between devices, exchange(): lax.all_to_all(value, ('shard', 'grp'), split_axis=0, concat_axis=0, tile...  27.3 us
    all_to_all x5, starting transfers between devices, exchange(): lax.all_to_all(value, ('shard', 'grp'), split_axis=0, concat_axis=0, tile...  24.4 us
    pallas_call x1, Pallas kernels, edges(): call(functools.partial(edges_kernel, parts=parts, pooled=pool is not None...  20.2 us
    pallas_call x1, Pallas kernels, spread(): call(functools.partial(spread_kernel, first=so_far is None), 'spread_rows...  19.3 us
    pallas_call x1, Pallas kernels, collect(): call(functools.partial(collect_kernel, group=group), 'collect_grads', 2 *...  18 us
  transfers between devices with their start and end apart: 17, of which 12 were waited for; matrix products, arithmetic and copies ran while one was open for 4% of the time, Pallas kernels for 33%

commit v1 on v0

--- a/solution.py
+++ b/solution.py
@@ -113,7 +113,7 @@
             place = (q ^ turn) * SHARE + rank
             slot_refs[0][at] = jnp.where(inside, owner * LANES + place, -1)
             places.append(jnp.where(inside, place, -1))
-        msg_ref[:, :LANES] = fill(members, codes, places, LANES)
+        msg_ref[:, 0, :LANES] = fill(members, codes, places, LANES)
         offset = LANES
 
         pool_ref, busy_ref = slot_refs[1:]
@@ -136,7 +136,7 @@
             places.append(jnp.where(inside, place, -1))
         listed = fill(spilled, spill_codes, places, 2 * LANES)
         for shard in range(shards):
-            msg_ref[shard * RELAYS : (shard + 1) * RELAYS, offset : offset + 2 * LANES] = (
+            msg_ref[shard * RELAYS : (shard + 1) * RELAYS, 0, offset : offset + 2 * LANES] = (
                 jnp.broadcast_to(listed[shard : shard + 1], (RELAYS, 2 * LANES))
             )
         offset += 2 * LANES
@@ -155,7 +155,8 @@
                 place = jnp.where((owner >= 0) & (place >= 0) & (place < LANES), place, -1)
                 slot_refs[chunk][at] = jnp.where(place >= 0, owner * LANES + place, -1)
                 places.append(place)
-            msg_ref[:, chunk * LANES : (chunk + 1) * LANES] = fill(members, codes, places, LANES)
+            listed = fill(members, codes, places, LANES)
+            msg_ref[:, 0, chunk * LANES : (chunk + 1) * LANES] = listed
         offset = chunks * LANES
 
     where, holder, codes, members = prepare([own_ref[b : b + 1, :] for b in range(spans)], part)
@@ -165,7 +166,7 @@
     places = [jnp.where(owner >= 0, rank, -1) for owner, rank in zip(holder, found)]
     listed = fill(members, codes, places, LANES)
     lanes = lax.broadcasted_iota(jnp.int32, listed.shape, 1)
-    msg_ref[:, offset:] = jnp.where(lanes == LANES - 1, flag, listed)
+    msg_ref[:, 0, offset:] = jnp.where(lanes == LANES - 1, flag, listed)
 
 
 def make_slots(me, src_ids, dst_ids, own, rows_dev, devices, chunks, neg_cap, width, part):
@@ -195,7 +196,7 @@
             pl.BlockSpec(dst_ids.shape, lambda: (0,)),
             pl.BlockSpec(own.shape, lambda: (0, 0)),
         ],
-        out_shape=[jax.ShapeDtypeStruct((devices, lanes), jnp.int32)]
+        out_shape=[jax.ShapeDtypeStruct((devices, 1, lanes), jnp.int32)]
         + slots
         + [jax.ShapeDtypeStruct((spans, part), jnp.int32)],
     )(me.reshape(1, 1), src_ids, dst_ids, own)
@@ -298,12 +299,11 @@
     return rows
 
 
-def gather_quarters_kernel(table_ref, req_ref, neg_req_ref, out_ref, *, neg_cap):
+def gather_quarters_kernel(table_ref, asked_ref, out_ref, *, neg_cap):
     feature, rows_dev = table_ref.shape
     group = out_ref.shape[0]
     share = rows_dev // PARTS
-    first = pl.program_id(0) * group
-    ids = [req_ref[pl.ds(first + i, 1), :] for i in range(group)]
+    ids = [asked_ref[i : i + 1, :LANES] for i in range(group)]
     found = []
     for part, row in enumerate(quarter_ids(ids)):
         start = part * share
@@ -316,27 +316,27 @@
         for j in range(1, PARTS):
             rows = jnp.where(lanes == j, found[j ^ (i % PARTS)][:, at], rows)
         out_ref[i, start:] = rows.astype(BF16)
-    row = [neg_req_ref[pl.ds(first + i, 1), :neg_cap] for i in range(group)]
+    negs = slice(asked_ref.shape[1] - LANES, asked_ref.shape[1] - LANES + neg_cap)
+    row = [asked_ref[i : i + 1, negs] for i in range(group)]
     neg = dot(table_ref[...], one_hot(rows_dev, jnp.concatenate(row, axis=1)), NN)
     pack_all(out_ref, 0, neg_cap, neg.T, neg)
 
 
-def gather_quarters(table, requests, neg_requests, neg_cap):
+def gather_quarters(table, asked, neg_cap):
     feature, rows_dev = table.shape
-    devices = requests.shape[0]
+    devices = asked.shape[0]
     group = 16
     height = feature + packed_height(neg_cap, feature)
-    whole = pl.BlockSpec((devices, LANES), lambda i: (0, 0))
     return call(
         functools.partial(gather_quarters_kernel, neg_cap=neg_cap),
         "gather_quarters",
         feature * rows_dev * devices * (LANES // 2 + 2 * neg_cap),
         2 * feature * (rows_dev + devices * (LANES + neg_cap)),
         grid=(devices // group,),
-        in_specs=[pl.BlockSpec((feature, rows_dev), lambda i: (0, 0)), whole, whole],
+        in_specs=[pl.BlockSpec((feature, rows_dev), lambda i: (0, 0)), pl.BlockSpec((group, asked.shape[1]), lambda i: (i, 0))],
         out_specs=pl.BlockSpec((group, height, LANES), lambda i: (i, 0, 0)),
         out_shape=jax.ShapeDtypeStruct((devices, height, LANES), BF16),
-    )(table, requests, neg_requests)
+    )(table, asked)
 
 
 def gather_pool_kernel(table_ref, req_ref, out_ref, *, group):
@@ -473,10 +473,10 @@
     flat_ref[pieces * LANES :] = jnp.concatenate(tails, axis=1).astype(BF16)
 
 
-def expand_pool(rows, busy, out_ref):
-    feature = rows.shape[1]
+def expand_pool(turned, busy, out_ref):
+    feature = turned.shape[0]
     pieces = feature // LANES
-    turned = rows.T
+    rows = turned.T
     out_ref[...] = jnp.zeros(out_ref.shape, out_ref.dtype)
     shards = out_ref.shape[0] // RELAYS
     for shard, relay, first, count, to in compact_places(shards):
@@ -551,9 +551,9 @@
     dst_grad = (pos_weight * product).astype(BF16)
     src_grad_ref[...] = src_grad
     dst_grad_ref[...] = dst_grad
-    neg_grad = dot(weight, query, NT)
+    neg_grad = dot(query, weight, NT).T
     if pooled:
-        pool_sums[...] += dot(src_hot, src_grad, NT) + dot(dst_hot, dst_grad, NT)
+        pool_sums[...] += dot(src_grad, src_hot, NT) + dot(dst_grad, dst_hot, NT)
 
     for k in range(parts):
         neg_grad_refs[k][0] = neg_grad[k * part : (k + 1) * part].astype(BF16)
@@ -601,7 +601,7 @@
         scratch += [
             pltpu.VMEM((count, feature // LANES * LANES), BF16),
             pltpu.VMEM((feature, count), BF16),
-            pltpu.VMEM((count, feature), F32),
+            pltpu.VMEM((feature, count), F32),
         ]
     src_grad, dst_grad, *rest = call(
         functools.partial(edges_kernel, parts=parts, pooled=pool is not None),
@@ -755,7 +755,7 @@
 
 
 def add_quarters_kernel(
-    recv_ref, req_ref, neg_req_ref, so_far_ref, out_ref, flat, neg_rows, neg_flat, *, neg_cap
+    recv_ref, asked_ref, so_far_ref, out_ref, flat, neg_rows, neg_flat, *, neg_cap
 ):
     devices = recv_ref.shape[0]
     feature, rows = out_ref.shape
@@ -774,20 +774,21 @@
         unpack_all(recv_ref, 0, neg_cap, neg_rows, neg_flat)
 
     base = step * rows
-    asked = quarter_ids([req_ref[d : d + 1, :] for d in range(devices)])
+    asked = quarter_ids([asked_ref[d : d + 1, :LANES] for d in range(devices)])
     row = asked[0]
     for part in range(1, PARTS):
         row = jnp.where(step == part, asked[part], row)
     total = dot(flat[step], one_hot(rows, row, base), NT)
-    row = jnp.concatenate([neg_req_ref[d : d + 1, :neg_cap] for d in range(devices)], axis=1)
+    negs = slice(asked_ref.shape[1] - LANES, asked_ref.shape[1] - LANES + neg_cap)
+    row = jnp.concatenate([asked_ref[d : d + 1, negs] for d in range(devices)], axis=1)
     out_ref[...] = total + dot(neg_flat[...], one_hot(rows, row, base), NT) + so_far_ref[...]
 
 
-def add_quarters(recv, requests, neg_requests, so_far, neg_cap):
+def add_quarters(recv, asked, so_far, neg_cap):
     feature, rows_dev = so_far.shape
     devices = recv.shape[0]
     slots = devices * LANES
-    whole_req = pl.BlockSpec((devices, LANES), lambda i: (0, 0))
+    whole_asked = pl.BlockSpec(asked.shape, lambda i: (0, 0))
     rows_spec = pl.BlockSpec((feature, rows_dev // PARTS), lambda i: (0, i))
     return call(
         functools.partial(add_quarters_kernel, neg_cap=neg_cap),
@@ -795,12 +796,12 @@
         feature * (slots // 2 + 2 * devices * neg_cap) * rows_dev,
         2 * feature * slots + 8 * feature * rows_dev,
         grid=(PARTS,),
-        in_specs=[pl.BlockSpec(recv.shape, lambda i: (0, 0, 0)), whole_req, whole_req, rows_spec],
+        in_specs=[pl.BlockSpec(recv.shape, lambda i: (0, 0, 0)), whole_asked, rows_spec],
         out_specs=rows_spec,
         out_shape=jax.ShapeDtypeStruct((feature, rows_dev), F32),
         scratch_shapes=[pltpu.VMEM((PARTS, feature, slots // PARTS), BF16)]
         + unpack_scratch(devices, neg_cap, feature),
-    )(recv, requests, neg_requests, so_far)
+    )(recv, asked, so_far)
 
 
 def add_pool_kernel(*refs, rows, first):
@@ -926,7 +927,7 @@
             width,
             part,
         )
-        asked = exchange(message)
+        asked = exchange(message)[:, 0]
         return asked, asked[:, -LANES:], slots, slots[-1]
 
     def chunked(zero):
@@ -949,11 +950,10 @@
 
     def pooled():
         asked, neg_asked, (slot, pool_slot, busy, _), neg_slot = ask(0, 0)
-        direct = asked[:, :LANES]
         listed = asked[:, LANES : LANES + RELAYS * POOL].reshape(devices, RELAYS, POOL)
         listed = listed.transpose(1, 0, 2).reshape(RELAYS, devices * POOL) - me * rows_dev
         listed = listed[me ^ jnp.arange(RELAYS, dtype=jnp.int32)]
-        back = exchange(gather_quarters(table, direct, neg_asked, neg_cap))
+        back = exchange(gather_quarters(table, asked, neg_cap))
         far = swap(gather_pool(table, listed[3], devices), 1)
         far = swap(gather_pool(table, listed[2], devices) + far, 2)
         near = swap(gather_pool(table, listed[1], devices), 1)
@@ -973,7 +973,7 @@
         grad = add_pool(near, swap(near, 1), listed[:2], None, feature, rows_dev)
         far = after(far, grad)
         grad = add_pool(far, swap(far, 1), listed[2:], grad, feature, rows_dev)
-        return add_quarters(sent, direct, neg_asked, grad, neg_cap), jnp.max(neg_asked[:, -1])
+        return add_quarters(sent, asked, grad, neg_cap), jnp.max(neg_asked[:, -1])
 
     if chunks == 1 or sharers != RELAYS:
         return chunked(0).T

time: 348 us -> 345 us (level)
    unnamed x32 -> x34, local copies, waits for them, and re-layouts: 7.09 us -> 7.71 us
where the time goes in v1:
time: 345 us; the launch traced here: 339 us
  Pallas kernels  163 us (47%)
  waiting for transfers between devices  120 us (35%)
  starting transfers between devices  33.7 us (10%)
  local copies, waits for them, and re-layouts  11.1 us (3%)
  other arithmetic  9.72 us (3%)
    ppermute x12, waiting for transfers between devices, swap(): return lax.ppermute(value, 'grp', [(i, i ^ bit) for i in range(sharers)])  92.7 us
    pallas_call x4, Pallas kernels, gather_pool(): call(functools.partial(gather_pool_kernel, group=group), 'gather_pool', 2...  37.1 us
    pallas_call x2, Pallas kernels, add_pool(): call(functools.partial(add_pool_kernel, rows=rows, first=so_far is None),...  31.5 us
    all_to_all x5, waiting for transfers between devices, exchange(): lax.all_to_all(value, ('shard', 'grp'), split_axis=0, concat_axis=0, tile...  27.2 us
    all_to_all x5, starting transfers between devices, exchange(): lax.all_to_all(value, ('shard', 'grp'), split_axis=0, concat_axis=0, tile...  24.6 us
    pallas_call x1, Pallas kernels, spread(): call(functools.partial(spread_kernel, first=so_far is None), 'spread_rows...  19.3 us
    pallas_call x1, Pallas kernels, edges(): call(functools.partial(edges_kernel, parts=parts, pooled=pool is not None...  19.3 us
    pallas_call x1, Pallas kernels, collect(): call(functools.partial(collect_kernel, group=group), 'collect_grads', 2 *...  18 us
  transfers between devices with their start and end apart: 17, of which 12 were waited for; matrix products, arithmetic and copies ran while one was open for 4% of the time, Pallas kernels for 33%

profile of v1, /device:TPU:0, one launch (start us, length us, event | category | flops | bytes accessed | tf_op | source)
XLA Modules:
  0.0 339.2 jit_solution(15152108732832709781)
XLA Ops:
  0.0 0.7 copy-done
  0.8 3.9 %slots.2 = (s32[32,1,512]{2,1,0:T(1,128)}, s32[4,1024]{1,0:T(4,128)}, s32[4,1024]{1,0:T(4,128)}, s32[1,1]{1,0:T(1,128)}, s32[2,256]{1,0:T(2,128)}) custom-call(s32[1,1]{1,0:T(1,128)} %bitcast.2.me_ref, s32[2000]{0:T(1024)} %src_ref.1, s32[2000]{0:T(1024)} %dst_ref.1, s32[2,250]{1,0:T(2,128)S(1)} %constant_dynamic-slice_fusion.own_ref), custom_call_target="tpu_custom_call" | custom-call | flops 268435456 | bytes 32768 | tf_op jit(solution)/shard_map/slots/pallas_call | solution.py:180
  4.7 7.3 %all-to-all-start.5 = ((s32[32,1,512]{2,1,0:T(1,128)}), s32[32,1,512]{2,1,0:T(1,128)S(1)}, u32[]{:S(2)}, u32[]{:S(2)}) async-start(s32[32,1,512]{2,1,0:T(1,128)} %get-tuple-element.68), calls=%async_computation.5 | async-start | bytes 131072 | tf_op jit(solution)/shard_map/all_to_all | solution.py:861
  12.0 3.3 convert_bitcast_fusion.table_ref
  15.3 4.1 %all-to-all-done.5 = s32[32,1,512]{2,1,0:T(1,128)S(1)} async-done(((s32[32,1,512]{2,1,0:T(1,128)}), s32[32,1,512]{2,1,0:T(1,128)S(1)}, u32[]{:S(2)}, u32[]{:S(2)}) %all-to-all-start.5) | async-done | bytes 65568 | tf_op jit(solution)/shard_map/all_to_all | solution.py:861
  19.4 0.6 copy.28
  20.0 11.5 %gather_quarters.1 = bf16[32,512,128]{2,1,0:T(8,128)(2,1)} custom-call(bf16[400,4096]{1,0:T(8,128)(2,1)S(1)} %convert_bitcast_fusion.table_ref, s32[32,512]{1,0:T(8,128)} %bitcast.26), custom_call_target="tpu_custom_call" | custom-call | flops 6710886400 | bytes 7372800 | tf_op jit(solution)/shard_map/gather_quarters/pallas_call | solution.py:330
  31.6 4.2 %all-to-all-start.6 = ((bf16[32,512,128]{2,1,0:T(8,128)(2,1)}), bf16[32,512,128]{2,1,0:T(8,128)(2,1)}, u32[]{:S(2)}, u32[]{:S(2)}) async-start(bf16[32,512,128]{2,1,0:T(8,128)(2,1)} %gather_quarters.1), calls=%async_computation.6 | async-start | bytes 8388608 | tf_op jit(solution)/shard_map/all_to_all | solution.py:861
  35.8 0.1 sub.17
  36.0 0.1 sub.19
  36.1 0.6 gather_fusion
  36.6 0.6 fusion.2
  37.3 9.2 %gather_pool.7 = bf16[32,160,128]{2,1,0:T(8,128)(2,1)} custom-call(bf16[400,4096]{1,0:T(8,128)(2,1)S(1)} %convert_bitcast_fusion.table_ref, s32[4,1,384]{2,1,0:T(1,128)} %bitcast.31), custom_call_target="tpu_custom_call" | custom-call | flops 5033164800 | bytes 4505600 | tf_op jit(solution)/shard_map/gather_pool/pallas_call | solution.py:354
  46.5 0.2 collective-permute-start.10
  46.7 9.3 %gather_pool.5 = bf16[32,160,128]{2,1,0:T(8,128)(2,1)} custom-call(bf16[400,4096]{1,0:T(8,128)(2,1)S(1)} %convert_bitcast_fusion.table_ref, s32[4,1,384]{2,1,0:T(1,128)} %bitcast.32), custom_call_target="tpu_custom_call" | custom-call | flops 5033164800 | bytes 4505600 | tf_op jit(solution)/shard_map/gather_pool/pallas_call | solution.py:354
  56.0 0.3 collective-permute-start.9
  56.3 9.3 %gather_pool.6 = bf16[32,160,128]{2,1,0:T(8,128)(2,1)} custom-call(bf16[400,4096]{1,0:T(8,128)(2,1)S(1)} %convert_bitcast_fusion.table_ref, s32[4,1,384]{2,1,0:T(1,128)} %bitcast.30), custom_call_target="tpu_custom_call" | custom-call | flops 5033164800 | bytes 4505600 | tf_op jit(solution)/shard_map/gather_pool/pallas_call | solution.py:354
  65.6 1.7 add.50
  67.3 1.8 collective-permute-start.11
  69.2 9.3 %gather_pool.4 = bf16[32,160,128]{2,1,0:T(8,128)(2,1)} custom-call(bf16[400,4096]{1,0:T(8,128)(2,1)S(1)} %convert_bitcast_fusion.table_ref, s32[4,1,384]{2,1,0:T(1,128)} %bitcast.33), custom_call_target="tpu_custom_call" | custom-call | flops 5033164800 | bytes 4505600 | tf_op jit(solution)/shard_map/gather_pool/pallas_call | solution.py:354
  78.4 32.7 %collective-permute-done.11 = bf16[32,160,128]{2,1,0:T(8,128)(2,1)S(1)} collective-permute-done((bf16[32,160,128]{2,1,0:T(8,128)(2,1)S(1)}, bf16[32,160,128]{2,1,0:T(8,128)(2,1)S(1)}, u32[]{:S(2)}, u32[]{:S(2)}) %collective-permute-start.11) | collective-permute-done | bytes 1310752 | tf_op jit(solution)/shard_map/ppermute | solution.py:866
  111.1 2.7 add_add_fusion
  113.8 16.1 %all-to-all-done.6.refs_0_.back_ref = bf16[32,512,128]{2,1,0:T(8,128)(2,1)} async-done(((bf16[32,512,128]{2,1,0:T(8,128)(2,1)}), bf16[32,512,128]{2,1,0:T(8,128)(2,1)}, u32[]{:S(2)}, u32[]{:S(2)}) %all-to-all-start.6) | async-done | bytes 4194336 | tf_op jit(solution)/shard_map/all_to_all | solution.py:861
  130.0 4.0 %all-to-all-start.7 = ((bf16[32,160,128]{2,1,0:T(8,128)(2,1)}), bf16[32,160,128]{2,1,0:T(8,128)(2,1)}, u32[]{:S(2)}, u32[]{:S(2)}) async-start(bf16[32,160,128]{2,1,0:T(8,128)(2,1)} %add_add_fusion), calls=%async_computation.7 | async-start | bytes 2621440 | tf_op jit(solution)/shard_map/all_to_all | solution.py:861
  133.9 0.6 reshape.50.refs_1_
  134.6 2.9 spread_negatives.2.refs_4_
  137.5 0.4 collective-permute-start.6
  137.8 1.7 collective-permute-start.7
  139.5 19.3 %spread_rows.3.other_ref.refs_0_.refs_1_ = bf16[400,4096]{1,0:T(8,128)(2,1)} custom-call(bf16[32,512,128]{2,1,0:T(8,128)(2,1)} %all-to-all-done.6.refs_0_.back_ref, s32[4,1,1024]{2,1,0:T(1,128)} %reshape.50.refs_1_), custom_call_target="tpu_custom_call" | custom-call | flops 13421772800 | bytes 6553600 | tf_op jit(solution)/shard_map/spread_rows/pallas_call | solution.py:424
  158.8 1.3 collective-permute-done.7.refs_6_
  160.1 0.8 copy-done.9
  160.9 0.8 copy.33.value_ref
  161.8 0.3 collective-permute-start.8
  162.2 0.6 reshape.52.refs_2_
  162.8 0.6 reshape.53.refs_9_.refs_10_
  163.4 2.8 all-to-all-done.7.refs_8_
  166.1 19.3 %edges.2 = (bf16[400,2048]{1,0:T(8,128)(2,1)}, bf16[400,2048]{1,0:T(8,128)(2,1)}, bf16[2,256,400]{2,1,0:T(8,128)(2,1)}, bf16[2,256,400]{2,1,0:T(8,128)(2,1)}, bf...) custom-call(bf16[400,4096]{1,0:T(8,128)(2,1)} %spread_rows.3.other_ref.refs_0_.refs_1_, ...), custom_call_target="tpu_custom_call" | custom-call | flops 5033164800 | bytes 9830400 | tf_op jit(solution)/shard_map/edges/pallas_call | solution.py:606
  185.4 4.5 %all-to-all-start.9 = ((bf16[32,160,128]{2,1,0:T(8,128)(2,1)}), bf16[32,160,128]{2,1,0:T(8,128)(2,1)}, u32[]{:S(2)}, u32[]{:S(2)}) async-start(bf16[32,160,128]{2,1,0:T(8,128)(2,1)} %get-tuple-element.79), calls=%async_computation.9 | async-start | bytes 2621440 | tf_op jit(solution)/shard_map/all_to_all | solution.py:861
  190.0 0.4 collective-permute-start.13
  190.4 0.1 collective-permute-start.12
  190.5 1.6 collective-permute-done.13
  192.1 1.2 add_convert_fusion.1
  193.3 1.9 collective-permute-start.14
  195.3 18.0 %collect_grads.3.sent_ref = bf16[32,512,128]{2,1,0:T(8,128)(2,1)} custom-call(bf16[400,2048]{1,0:T(8,128)(2,1)} %get-tuple-element.73.src_ref, bf16[400,2048]{1,0:T(8,128)(2,1)} %get-tuple-element.74.dst_ref, s32[4,1024]{1,0:T(4,128)} %get-tuple-element.69.slot_ref), custom_call_target="tpu_custom_call" | custom-call | flops 13421772800 | bytes 6553600 | tf_op jit(solution)/shard_map/collect_grads/pallas_call | solution.py:642
  213.3 2.9 collective-permute-done.14.refs_2_
  216.2 0.8 copy-done.11
  217.0 3.5 %collect_negatives.2 = bf16[32,512,128]{2,1,0:T(8,128)(2,1)} custom-call(bf16[32,512,128]{2,1,0:T(8,128)(2,1)} %collect_grads.3.sent_ref, s32[2,256]{1,0:T(2,128)} %get-tuple-element.70.slot_ref, bf16[2,256,400]{2,1,0:T(8,128)(2,1)} %get-tuple-element.75.refs_0_, bf16[2,256,400]{2,1,0:T(8,128)(2,1)} %copy-done.10, ...), custom_call_target="tpu_custom_call", output_to_operand_aliasing={{}: (0, {})} | custom-call | flops 419430400 | bytes 2457600 | tf_op jit(solution)/shard_map/collect_negatives/pallas_call | solution.py:677
  220.5 1.6 all-to-all-done.9.refs_0_
  222.2 4.5 %all-to-all-start.8 = ((bf16[32,512,128]{2,1,0:T(8,128)(2,1)}), bf16[32,512,128]{2,1,0:T(8,128)(2,1)}, u32[]{:S(2)}, u32[]{:S(2)}) async-start(bf16[32,512,128]{2,1,0:T(8,128)(2,1)} %collect_negatives.2), calls=%async_computation.8 | async-start | bytes 8388608 | tf_op jit(solution)/shard_map/all_to_all | solution.py:861
  226.7 0.2 collective-permute-start.16
  227.0 1.7 collective-permute-start.15
  228.6 1.4 collective-permute-done.16.refs_1_
  230.0 1.1 copy-done.21
  231.1 15.5 %add_pool.2.other_ref.refs_4_ = f32[400,4096]{1,0:T(8,128)} custom-call(bf16[32,160,128]{2,1,0:T(8,128)(2,1)} %all-to-all-done.9.refs_0_, bf16[32,160,128]{2,1,0:T(8,128)(2,1)} %copy-done.21, s32[1,1536]{1,0:T(1,128)} %get-tuple-element.104.refs_2_, s32[1,1536]{1,0:T(1,128)} %get-tuple-element.102.refs_3_), custom_call_target="tpu_custom_call" | custom-call | flops 10066329600 | bytes 9011200 | tf_op jit(solution)/shard_map/add_pool/pallas_call | solution.py:833
  246.6 50.2 %collective-permute-done.15.value_ref = bf16[32,160,128]{2,1,0:T(8,128)(2,1)S(1)} collective-permute-done((bf16[32,160,128]{2,1,0:T(8,128)(2,1)}, bf16[32,160,128]{2,1,0:T(8,128)(2,1)S(1)}, u32[]{:S(2)}, u32[]{:S(2)}) %collective-permute-start.15) | collective-permute-done | bytes 1310752 | tf_op jit(solution)/shard_map/ppermute | solution.py:866
  296.9 1.1 copy-done.8
  297.9 0.7 slice_reduce_fusion
  298.7 2.5 collective-permute-done.17.refs_1_
  301.2 1.1 copy-done.22
  302.2 16.0 %add_pool.3.so_far_ref = f32[400,4096]{1,0:T(8,128)} custom-call(bf16[32,160,128]{2,1,0:T(8,128)(2,1)} %after.3.refs_0_, bf16[32,160,128]{2,1,0:T(8,128)(2,1)} %copy-done.22, s32[1,1536]{1,0:T(1,128)} %get-tuple-element.103.refs_2_, s32[1,1536]{1,0:T(1,128)} %get-tuple-element.105.refs_3_, f32[400,4096]{1,0:T(8,128)} %add_pool.2.other_ref.refs_4_), custom_call_target="tpu_custom_call" | custom-call | flops 10066329600 | bytes 9011200 | tf_op jit(solution)/shard_map/add_pool/pallas_call | solution.py:833
  318.3 2.6 all-to-all-done.8.recv_ref
  320.8 15.6 %add_quarters.1 = f32[400,4096]{1,0:T(8,128)} custom-call(bf16[32,512,128]{2,1,0:T(8,128)(2,1)} %all-to-all-done.8.recv_ref, s32[32,512]{1,0:T(8,128)} %bitcast.27, f32[400,4096]{1,0:T(8,128)} %add_pool.3.so_far_ref), custom_call_target="tpu_custom_call" | custom-call | flops 6710886400 | bytes 16384000 | tf_op jit(solution)/shard_map/add_quarters/pallas_call | solution.py:793
  336.4 1.7 while.11
  338.1 0.7 copy-done.1
  (41 shorter events, 0.3 us)
Async XLA Ops:
  0.0 0.7 copy-start
  4.7 14.7 %all-to-all-start.5 = ((s32[32,1,512]{2,1,0:T(1,128)}), s32[32,1,512]{2,1,0:T(1,128)S(1)}, u32[]{:S(2)}, u32[]{:S(2)}) async-start(s32[32,1,512]{2,1,0:T(1,128)} %get-tuple-element.68), calls=%async_computation.5 | async-start | bytes 131072 | tf_op jit(solution)/shard_map/all_to_all | solution.py:861
  31.6 4.3 %copy-start.16 = (s32[32,1,512]{2,0,1:T(8,128)S(1)}, s32[32,1,512]{2,0,1:T(8,128)}, u32[]{:S(2)}) copy-start(s32[32,1,512]{2,0,1:T(8,128)} %copy.28) | copy-start | bytes 196612
  31.6 98.4 %all-to-all-start.6 = ((bf16[32,512,128]{2,1,0:T(8,128)(2,1)}), bf16[32,512,128]{2,1,0:T(8,128)(2,1)}, u32[]{:S(2)}, u32[]{:S(2)}) async-start(bf16[32,512,128]{2,1,0:T(8,128)(2,1)} %gather_quarters.1), calls=%async_computation.6 | async-start | bytes 8388608 | tf_op jit(solution)/shard_map/all_to_all | solution.py:861
  46.5 19.1 %collective-permute-start.10 = (bf16[32,160,128]{2,1,0:T(8,128)(2,1)}, bf16[32,160,128]{2,1,0:T(8,128)(2,1)S(1)}, u32[]{:S(2)}, u32[]{:S(2)}) collective-permute-start(bf16[32,160,128]{2,1,0:T(8,128)(2,1)} %gather_pool.7), channel_id=1, source_target_pairs={{0,1},{1,0},{2,3},{3,2},{4,5},{5,4},{6,7},{7,6},{8,9},{9,8},{10,11... | collective-permute-start | bytes 3932168 | tf_op jit(solution)/shard_map/ppermute | solution.py:866
  56.0 22.4 %collective-permute-start.9 = (bf16[32,160,128]{2,1,0:T(8,128)(2,1)}, bf16[32,160,128]{2,1,0:T(8,128)(2,1)S(1)}, u32[]{:S(2)}, u32[]{:S(2)}) collective-permute-start(bf16[32,160,128]{2,1,0:T(8,128)(2,1)} %gather_pool.5), channel_id=1, source_target_pairs={{0,1},{1,0},{2,3},{3,2},{4,5},{5,4},{6,7},{7,6},{8,9},{9,8},{10,11... | collective-permute-start | bytes 3932168 | tf_op jit(solution)/shard_map/ppermute | solution.py:866
  67.3 43.8 %collective-permute-start.11 = (bf16[32,160,128]{2,1,0:T(8,128)(2,1)S(1)}, bf16[32,160,128]{2,1,0:T(8,128)(2,1)S(1)}, u32[]{:S(2)}, u32[]{:S(2)}) collective-permute-start(bf16[32,160,128]{2,1,0:T(8,128)(2,1)S(1)} %add.50), channel_id=1, source_target_pairs={{0,2},{1,3},{2,0},{3,1},{4,6},{5,7},{6,4},{7,5},{8,10},{9,11},{10,... | collective-permute-start | bytes 3932168 | tf_op jit(solution)/shard_map/ppermute | solution.py:866
  78.4 55.5 %copy-start.18 = (s32[4,1024]{1,0:T(4,128)S(1)}, s32[4,1024]{1,0:T(4,128)}, u32[]{:S(2)}) copy-start(s32[4,1024]{1,0:T(4,128)} %get-tuple-element.69.slot_ref) | copy-start | bytes 49156
  130.0 36.2 %all-to-all-start.7 = ((bf16[32,160,128]{2,1,0:T(8,128)(2,1)}), bf16[32,160,128]{2,1,0:T(8,128)(2,1)}, u32[]{:S(2)}, u32[]{:S(2)}) async-start(bf16[32,160,128]{2,1,0:T(8,128)(2,1)} %add_add_fusion), calls=%async_computation.7 | async-start | bytes 2621440 | tf_op jit(solution)/shard_map/all_to_all | solution.py:861
  137.5 28.7 %collective-permute-start.6 = (bf16[2,256,400]{2,1,0:T(8,128)(2,1)}, bf16[2,256,400]{2,1,0:T(8,128)(2,1)}, u32[]{:S(2)}, u32[]{:S(2)}) collective-permute-start(bf16[2,256,400]{2,1,0:T(8,128)(2,1)} %spread_negatives.2.refs_4_), channel_id=1, source_target_pairs={{0,1},{1,0},{2,3},{3,2},{4,5},{5,4},{6,7},{7,6},{8,9},{9,8},{10,11... | collective-permute-start | bytes 1228808 | tf_op jit(solution)/shard_map/ppermute | solution.py:866
  137.8 22.3 %collective-permute-start.7 = (bf16[2,256,400]{2,1,0:T(8,128)(2,1)}, bf16[2,256,400]{2,1,0:T(8,128)(2,1)S(1)}, u32[]{:S(2)}, u32[]{:S(2)}) collective-permute-start(bf16[2,256,400]{2,1,0:T(8,128)(2,1)} %spread_negatives.2.refs_4_), channel_id=1, source_target_pairs={{0,2},{1,3},{2,0},{3,1},{4,6},{5,7},{6,4},{7,5},{8,10},{9,11},{10,... | collective-permute-start | bytes 1228808 | tf_op jit(solution)/shard_map/ppermute | solution.py:866
  158.8 3.3 copy-start.20
  158.8 4.0 %copy-start.19 = (s32[4,1024]{1,0:T(4,128)S(1)}, s32[4,1024]{1,0:T(4,128)}, u32[]{:S(2)}) copy-start(s32[4,1024]{1,0:T(4,128)} %get-tuple-element.71) | copy-start | bytes 49156
  160.1 0.8 copy-start.9
  161.8 4.4 %collective-permute-start.8 = (bf16[2,256,400]{2,1,0:T(8,128)(2,1)}, bf16[2,256,400]{2,1,0:T(8,128)(2,1)}, u32[]{:S(2)}, u32[]{:S(2)}) collective-permute-start(bf16[2,256,400]{2,1,0:T(8,128)(2,1)} %after.2), channel_id=1, source_target_pairs={{0,1},{1,0},{2,3},{3,2},{4,5},{5,4},{6,7},{7,6},{8,9},{9,8},{10,11... | collective-permute-start | bytes 1228808 | tf_op jit(solution)/shard_map/ppermute | solution.py:866
  162.2 135.8 %copy-start.17 = (s32[2,1024]{1,0:T(2,128)}, s32[2,1024]{1,0:T(2,128)S(1)}, u32[]{:S(2)}) copy-start(s32[2,1024]{1,0:T(2,128)S(1)} %pad.4) | copy-start | bytes 24580
  185.4 36.7 %all-to-all-start.9 = ((bf16[32,160,128]{2,1,0:T(8,128)(2,1)}), bf16[32,160,128]{2,1,0:T(8,128)(2,1)}, u32[]{:S(2)}, u32[]{:S(2)}) async-start(bf16[32,160,128]{2,1,0:T(8,128)(2,1)} %get-tuple-element.79), calls=%async_computation.9 | async-start | bytes 2621440 | tf_op jit(solution)/shard_map/all_to_all | solution.py:861
  190.0 2.2 collective-permute-start.13
  190.4 22.9 %collective-permute-start.12 = (bf16[2,256,400]{2,1,0:T(8,128)(2,1)}, bf16[2,256,400]{2,1,0:T(8,128)(2,1)S(1)}, u32[]{:S(2)}, u32[]{:S(2)}) collective-permute-start(bf16[2,256,400]{2,1,0:T(8,128)(2,1)} %get-tuple-element.76), channel_id=1, source_target_pairs={{0,1},{1,0},{2,3},{3,2},{4,5},{5,4},{6,7},{7,6},{8,9},{9,8},{10,11... | collective-permute-start | bytes 1228808 | tf_op jit(solution)/shard_map/ppermute | solution.py:866
  193.3 22.9 %collective-permute-start.14 = (bf16[2,256,400]{2,1,0:T(8,128)(2,1)S(1)}, bf16[2,256,400]{2,1,0:T(8,128)(2,1)S(1)}, u32[]{:S(2)}, u32[]{:S(2)}) collective-permute-start(bf16[2,256,400]{2,1,0:T(8,128)(2,1)S(1)} %add_convert_fusion.1), channel_id=1, source_target_pairs={{0,2},{1,3},{2,0},{3,1},{4,6},{5,7},{6,4},{7,5},{8,10},{9,11},{10,... | collective-permute-start | bytes 1228808 | tf_op jit(solution)/shard_map/ppermute | solution.py:866
  213.3 3.0 copy-start.10
  216.2 0.8 copy-start.11
  222.2 98.7 %all-to-all-start.8 = ((bf16[32,512,128]{2,1,0:T(8,128)(2,1)}), bf16[32,512,128]{2,1,0:T(8,128)(2,1)}, u32[]{:S(2)}, u32[]{:S(2)}) async-start(bf16[32,512,128]{2,1,0:T(8,128)(2,1)} %collect_negatives.2), calls=%async_computation.8 | async-start | bytes 8388608 | tf_op jit(solution)/shard_map/all_to_all | solution.py:861
  226.7 3.3 collective-permute-start.16
  227.0 69.9 %collective-permute-start.15 = (bf16[32,160,128]{2,1,0:T(8,128)(2,1)}, bf16[32,160,128]{2,1,0:T(8,128)(2,1)S(1)}, u32[]{:S(2)}, u32[]{:S(2)}) collective-permute-start(bf16[32,160,128]{2,1,0:T(8,128)(2,1)} %all-to-all-done.9.refs_0_), channel_id=1, source_target_pairs={{0,2},{1,3},{2,0},{3,1},{4,6},{5,7},{6,4},{7,5},{8,10},{9,11},{10,... | collective-permute-start | bytes 3932168 | tf_op jit(solution)/shard_map/ppermute | solution.py:866
  230.0 1.1 copy-start.21
  296.9 1.1 copy-start.8
  297.9 3.2 collective-permute-start.17
  301.2 1.1 copy-start.22
  318.2 18.2 %copy-start.14 = (s32[2000]{0:T(1024)S(1)}, s32[2000]{0:T(1024)}, u32[]{:S(2)}) copy-start(s32[2000]{0:T(1024)} %src_ref.1) | copy-start | bytes 24004
  318.2 18.2 %copy-start.15 = (s32[2000]{0:T(1024)S(1)}, s32[2000]{0:T(1024)}, u32[]{:S(2)}) copy-start(s32[2000]{0:T(1024)} %dst_ref.1) | copy-start | bytes 24004
  318.2 18.2 %copy-start.23 = (f32[64,400]{1,0:T(8,128)S(1)}, f32[64,400]{1,0:T(8,128)}, u32[]{:S(2)}) copy-start(f32[64,400]{1,0:T(8,128)} %refs_3_.1) | copy-start | bytes 307204
  338.1 0.7 copy-start.1
